TPU v7x, 32 devices: a whole 2x2x4 slice. The times are simulated.
32 devices in a mesh: wide: 8 (over z, x), batch: 4 (over y, core).
Axes of the slice: x: 2, y: 2, z: 4, core: 2. Of those that a mesh axis runs over, the one named last changes fastest.
Arguments:
- pooled: bfloat16 [2, 9216, 4096], P(None, 'wide', 'batch'), may hold values from -6 to 6
- weight: bfloat16 [2, 9216, 4096], P(None, 'wide'), may hold values from -0.09375 to 0.09375
- fc_bias: float32 [2, 4096], P(None, 'wide'), may hold values from -3 to 3
- stitch: float32 [2, 2, 4096], P(None, None, 'wide'), as said below
- cotangent: bfloat16 [2, 4096, 4096], P(None, 'wide', 'batch'), may hold values from -6 to 6
- valid_mask: int32 [9216], P('wide'), may hold values from 0 to 1, as said below
- image_group: int32 [4096], P('batch'), may hold values 0 or 1
- step_rate: float32 [1], replicated, may hold values from 0.004 to 0.02
Outputs:
- stitched: bfloat16 [2, 4096, 4096], P(None, 'wide', 'batch')
- pooled_grad: bfloat16 [2, 9216, 4096], P(None, 'wide', 'batch')
- weight_grad: float32 [2, 9216, 4096], P(None, 'wide', 'batch')
- bias_grad: float32 [2, 4096], P(None, ('wide', 'batch'))
- stitch_grad: float32 [2, 2, 4096], P(None, None, ('wide', 'batch'))
- stitch_new: float32 [2, 2, 4096], P(None, None, ('wide', 'batch'))
Inputs may be any that keep to these rules, and one draw needn't show every extreme that they name: valid_mask[k] depends only on k mod 36: it is 1 at 25 of the 36 pooled positions and 0 at the others. `stitch`: diagonal values lie in 0.6 to 1.2, off-diagonal ones in 0 to 0.4.
All inputs are finite; a program needn't handle non-finite values. No bound on the sum of `image_group` on one device may be relied on, other than what follows from the above.
Results may differ from a plain program's by a relative error of at most 0.0049.
Values may be sent and summed in bfloat16 or wider, within the bound.
A program may use at most 192 MiB of HBM per device.

v0:
```python
import jax
import jax.numpy as jnp
from jax import lax
from jax.sharding import PartitionSpec as P


def gelu_local(values):
    return jax.nn.gelu(values, approximate=True)


def body(pooled, weight, fc_bias, stitch, cotangent, valid_mask, image_group, step_rate):
    highest = lax.Precision.HIGHEST
    factor_f = 1.0 - image_group[None, :].astype(jnp.float32) * (
        1.0 - valid_mask[:, None].astype(jnp.float32)
    )
    masked = pooled * factor_f.astype(jnp.bfloat16)[None]
    owned = weight.shape[2] // lax.axis_size("wide")
    picked = weight
    summed = lax.psum_scatter(
        jnp.einsum("tkc,tkb->ctb", picked, masked, preferred_element_type=jnp.float32),
        "wide",
        scatter_dimension=0,
        tiled=True,
    )
    pre_act = summed + jnp.transpose(fc_bias)[:, :, None]
    hidden, gelu_back = jax.vjp(gelu_local, pre_act)
    stitched = jnp.einsum("ijc,cjb->icb", stitch, hidden, precision=highest)
    upstream = cotangent.astype(jnp.float32)
    stitch_part = jnp.einsum("icb,cjb->ijc", upstream, hidden, precision=highest)
    hidden_grad = jnp.einsum("ijc,icb->cjb", stitch, upstream, precision=highest)
    pre_grad = gelu_back(hidden_grad)[0]
    bias_part = jnp.transpose(jnp.sum(pre_grad, axis=2))
    pre_low = pre_grad.astype(jnp.bfloat16)
    bias_grad, stitch_grad = (
        lax.psum_scatter(bias_part, "batch", scatter_dimension=1, tiled=True),
        lax.psum_scatter(stitch_part, "batch", scatter_dimension=2, tiled=True),
    )
    portion = lax.all_gather(pre_low, "wide", axis=0, tiled=True)
    picked = weight
    input_sum = jnp.einsum("tkc,ctb->tkb", picked, portion, preferred_element_type=jnp.float32)
    block_grad = jnp.einsum("tkb,ctb->tkc", masked, portion, preferred_element_type=jnp.float32)
    weight_sum = block_grad
    input_sum, weight_sum = (input_sum, weight_sum)
    pooled_grad = (input_sum * factor_f[None]).astype(jnp.bfloat16)
    weight_grad = lax.psum_scatter(weight_sum, "batch", scatter_dimension=2, tiled=True)
    share = owned // lax.axis_size("batch")
    stitch_mine = lax.dynamic_slice_in_dim(stitch, lax.axis_index("batch") * share, share, 2)
    stitch_new = stitch_mine - step_rate[0] * stitch_grad
    return (
        stitched.astype(jnp.bfloat16),
        pooled_grad,
        weight_grad,
        bias_grad,
        stitch_grad,
        stitch_new,
    )


def solution(mesh):
    return jax.shard_map(
        body,
        mesh=mesh,
        in_specs=(
            P(None, "wide", "batch"),
            P(None, "wide", None),
            P(None, "wide"),
            P(None, None, "wide"),
            P(None, "wide", "batch"),
            P("wide"),
            P("batch"),
            P(),
        ),
        out_specs=(
            P(None, "wide", "batch"),
            P(None, "wide", "batch"),
            P(None, "wide", "batch"),
            P(None, ("wide", "batch")),
            P(None, None, ("wide", "batch")),
            P(None, None, ("wide", "batch")),
        ),
        check_vma=False,
    )
```

profile of v0, /device:TPU:0, one launch (start us, length us, event | category | flops | bytes accessed | tf_op | source)
XLA Modules:
  0.0 1128.4 jit_solution(2839872014449193954)
XLA Ops:
  7.2 0.0 reduce-scatter.6.cloned.1.call-start
  7.2 0.8 convert_element_type.28
  8.1 0.7 convert_subtract_fusion
  8.8 3.5 multiply_subtract_fusion
  12.3 4.3 copy.30
  16.6 30.5 %convolution_bitcast_fusion = f32[4096,2,1024]{0,2,1:T(8,128)} fusion(bf16[2,1152,4096]{2,1,0:T(8,128)(2,1)} %param.9, bf16[2,1152,1024]{2,1,0:T(8,128)(2,1)} %param.8, bf16[1152,1024]{1,0:T(8,128)(2,1)} %copy.30), kind=kOutput, calls=%fused_computation | convolution fusion | flops 19329712128 | bytes 59506688 | tf_op jit(solution)/shard_map/tkc,tkb->ctb/dot_general | solution.py:20
  47.1 0.6 all-gather.2.cloned.1.call-start
  47.6 0.1 copy-done.2
  47.7 0.3 copy.34
  48.0 9.5 fusion.15
  57.5 7.3 copy.36
  64.8 528.3 %reduce-scatter.6.cloned.1.call-done = f32[512,2,1024]{0,2,1:T(8,128)} async-done(((f32[4096,2,1024]{0,2,1:T(8,128)}), f32[512,2,1024]{0,2,1:T(8,128)}) %reduce-scatter.6.cloned.1.call-update) | async-done | bytes 4194320 | tf_op jit(solution)/shard_map/reduce_scatter | solution.py:19
  593.0 7.1 fusion.17
  600.2 0.0 reduce-scatter.10.cloned.1.call-start
  600.3 0.9 copy.48
  601.1 0.2 reduce-scatter.8.cloned.1.call-start
  601.4 225.7 %all-gather.2.cloned.1.call-done = bf16[4096,2,1024]{0,2,1:T(8,128)(2,1)} async-done(((bf16[512,2,1024]{0,2,1:T(8,128)(2,1)}), bf16[4096,2,1024]{0,2,1:T(8,128)(2,1)}) %all-gather.2.cloned.1.call-update) | async-done | bytes 16777232 | tf_op jit(solution)/shard_map/all_gather | solution.py:38
  827.1 28.5 %fusion.7 = f32[2,1152,4096]{2,1,0:T(8,128)} fusion(bf16[4096,2,1024]{0,2,1:T(8,128)(2,1)} %all-gather.2.cloned.1.call-done, bf16[2,1152,1024]{2,1,0:T(8,128)(2,1)} %param.8, bf16[1152,1024]{1,0:T(8,128)(2,1)} %copy.30), kind=kOutput, calls=%fused_computation.12 | convolution fusion | flops 19329712128 | bytes 61603840 | tf_op jit(solution)/shard_map/tkb,ctb->tkc/dot_general | solution.py:41
  856.3 0.6 dynamic-slice
  857.5 7.8 copy.32
  865.3 17.8 %fusion.10 = bf16[2,512,1024]{2,0,1:T(2,128)(2,1)S(1)} fusion(f32[512,2,1024]{2,1,0:T(2,128)} %copy.32, f32[2,2,512]{0,1,2:T(2,128)S(1)} %copy.34), kind=kOutput, calls=%fused_computation.17 | convolution fusion | flops 26214400 | bytes 6299648 | tf_op jit(solution)/shard_map/ijc,cjb->icb/dot_general | solution.py:27
  883.1 1.9 copy.42
  885.1 1.9 copy-done.1
  887.0 16.9 %convolution_bitcast_fusion.1 = f32[2,2,512]{0,1,2:T(2,128)} fusion(f32[512,2,1024]{2,1,0:T(2,128)S(1)} %copy-done.1, bf16[2,512,1024]{2,1,0:T(8,128)(2,1)S(1)} %copy-done), kind=kOutput, calls=%fused_computation.21 | convolution fusion | flops 25165824 | bytes 6299648 | tf_op jit(solution)/shard_map/icb,cjb->ijc/dot_general | solution.py:29
  904.0 24.3 %all-reduce = f32[2,2,512]{0,1,2:T(2,128)S(1)} all-reduce(f32[2,2,512]{0,1,2:T(2,128)} %convolution_bitcast_fusion.1), channel_id=5, replica_groups=mesh['wide'=8,'batch'=4] {'batch'}, use_global_device_ids=true, to_apply=%region_4.0.clone | all-reduce | flops 2048 | bytes 16384
  928.3 0.1 multiply_subtract_fusion.1
  928.4 0.7 copy.45
  929.0 0.7 copy.44
  929.7 1.5 copy.49
  931.2 31.3 %fusion = bf16[2,1152,1024]{1,2,0:T(8,128)(2,1)} fusion(bf16[4096,2,1024]{0,2,1:T(8,128)(2,1)} %all-gather.2.cloned.1.call-done, bf16[2,1152,4096]{2,1,0:T(8,128)(2,1)} %param.9, f32[1152,1024]{0,1:T(8,128)} %get-tuple-element.23), kind=kOutput, calls=%fused_computation.2 | convolution fusion | flops 19332071424 | bytes 45088768 | tf_op jit(solution)/shard_map/tkc,ctb->tkb/dot_general | solution.py:40
  962.5 6.7 copy.43
  969.2 152.5 %reduce-scatter.8.cloned.1.call-done = f32[2,1152,1024]{2,1,0:T(8,128)} async-done(((f32[2,1152,4096]{2,1,0:T(8,128)}), f32[2,1152,1024]{2,1,0:T(8,128)}) %reduce-scatter.8.cloned.1.call-update) | async-done | bytes 9437200 | tf_op jit(solution)/shard_map/reduce_scatter | solution.py:45
  (13 shorter events, 0.1 us)
Async XLA Ops:
  7.2 40.8 %copy-start = (bf16[2,512,1024]{2,1,0:T(8,128)(2,1)S(1)}, bf16[2,512,1024]{2,1,0:T(8,128)(2,1)}, u32[]{:S(2)}) copy-start(bf16[2,512,1024]{2,1,0:T(8,128)(2,1)} %param.12) | copy-start | bytes 6291460
  7.2 585.8 %reduce-scatter.6.cloned.1.call-start = ((), (), s32[]{:S(2)}) async-start(), calls=%async_computation.3 | async-start | bytes 37748736 | tf_op jit(solution)/shard_map/reduce_scatter | solution.py:19
  47.0 0.7 copy-start.2
  47.1 780.0 %all-gather.2.cloned.1.call-start = ((), (), s32[]{:S(2)}) async-start(), calls=%async_computation.4 | async-start | bytes 18874368 | tf_op jit(solution)/shard_map/all_gather | solution.py:38
  57.5 535.6 %copy-start.3 = (f32[2,512]{1,0:T(2,128)S(1)}, f32[2,512]{1,0:T(2,128)}, u32[]{:S(2)}) copy-start(f32[2,512]{1,0:T(2,128)} %param.10) | copy-start | bytes 12292
  600.2 329.5 %reduce-scatter.10.cloned.1.call-start = ((), (), s32[]{:S(2)}) async-start(), calls=%async_computation.6 | async-start | bytes 327680
  601.1 520.5 %reduce-scatter.8.cloned.1.call-start = ((), (), s32[]{:S(2)}) async-start(), calls=%async_computation.5 | async-start | bytes 47185920 | tf_op jit(solution)/shard_map/reduce_scatter | solution.py:45
  855.6 0.7 copy-start.4
  883.1 3.9 copy-start.1
Sparse Core Ops, SparseCore 0:
  47.2 545.7 reduce-scatter.5
  600.3 226.7 all-gather.1
  829.6 18.2 reduce-scatter.9
  855.7 265.8 reduce-scatter.7
where the time goes:
time: 1130 us
  waiting for transfers between devices  907 us (80%)
  matrix products  134 us (12%)
  local copies, waits for them, and re-layouts  34.5 us (3%)
  blocking collectives  24.3 us (2%)
  between operations  15.4 us (1%)
  other arithmetic  12.3 us (1%)
    reduce_scatter x1, waiting for transfers between devices, body(): lax.psum_scatter(jnp.einsum('tkc,tkb->ctb', picked, masked, preferred_ele...  528 us
    all_gather x1, waiting for transfers between devices, body(): portion = lax.all_gather(pre_low, 'wide', axis=0, tiled=True)  226 us
    reduce_scatter x1, waiting for transfers between devices, body(): lax.psum_scatter(weight_sum, 'batch', scatter_dimension=2, tiled=True)  152 us
    dot_general x1, matrix products, body(): jnp.einsum('tkc,ctb->tkb', picked, portion, preferred_element_type=jnp.fl...  31.3 us
    dot_general x1, matrix products, body(): jnp.einsum('tkc,tkb->ctb', picked, masked, preferred_element_type=jnp.flo...  30.5 us
    dot_general x1, matrix products, body(): jnp.einsum('tkb,ctb->tkc', masked, portion, preferred_element_type=jnp.fl...  28.5 us
    unnamed x1, blocking collectives  24.3 us
  transfers between devices with their start and end apart: 4, of which 3 were waited for; matrix products, arithmetic and copies ran while one was open for 12% of the time, Pallas kernels for 0%

commit v1 on v0

v1 whole, which is shorter than its diff:
```python
import functools
import math

import jax
import jax.numpy as jnp
from jax import lax
from jax.experimental import pallas as pl
from jax.experimental.pallas import tpu as pltpu
from jax.sharding import PartitionSpec as P

MESH = pl.DeviceIdType.MESH
BLK = 128
NZ, NX = 4, 2
F32, BF16 = jnp.float32, jnp.bfloat16
NT = (((1,), (1,)), ((), ()))
ROOT = math.sqrt(2.0 / math.pi)
CUBE = 0.044715
PIECES = 3


class Dims:
    def __init__(self, pooled, weight, cotangent):
        self.towers, self.feats, self.images = pooled.shape
        self.chans = weight.shape[2]
        self.own = cotangent.shape[1]
        self.subs = self.own // BLK
        self.parts = 2
        self.rows = self.images // self.parts
        self.rx = (self.rows * 19 // 32) // 16 * 16
        self.rz = self.rows - self.rx
        self.units = self.towers * self.subs * self.parts
        self.cols = NZ * NX * BLK
        self.third = self.feats // PIECES


def chunks(count, size=64):
    return [(r, min(size, count - r)) for r in range(0, count, size)]


def kernel(
    dm,
    step_ref, w_hbm, xm_hbm, xt_hbm, cot, bias, st, st8,
    out_s, pg_hbm, wg_hbm, out_small, xp_hbm,
    wb, xt, xb, xpb, acc, fwd, gat, gatp,
    x1_s, x1_r, xr_s, xr_r, zr_s, zr_r, zown, z2_s, z2_r,
    own, y_s, y_r, hid0, htmp, pgb, sacc, sum_s, sum_r,
    m_w, m_ld, m_x1s, m_x1r, m_xrs, m_xrr, m_zrs, m_zrr, m_z2s, m_z2r, m_z4s, m_z4r,
    m_gxs, m_gxr, m_gzs, m_gzr, m_x5s, m_x5r, m_cs, m_cr, m_ys, m_yr, m_ss, m_sr, m_xps, m_xpr, m_own, m_pg,
):
    n_units, rows, rx, rz = dm.units, dm.rows, dm.rx, dm.rz
    wi, bi = lax.axis_index("wide"), lax.axis_index("batch")
    z, x = wi // NX, wi % NX
    y, core = bi // 2, bi % 2
    x_dev = (z * NX + 1 - x, bi)
    c_dev = (wi, y * 2 + 1 - core)
    y_dev = (wi, (1 - y) * 2 + core)

    def z_dev(d):
        return (wi + NX, bi) if d == 0 else (wi - NX, bi)

    def far(d):
        return z if d == 0 else NZ - 1 - z

    def rc(src, dst, ss, rs, dev):
        return pltpu.make_async_remote_copy(src, dst, ss, rs, device_id=dev, device_id_type=MESH)

    def al(v, k=BLK):
        return pl.multiple_of(v, k)

    def tower(n):
        return n // (dm.subs * dm.parts)

    def sub(n):
        return (n // dm.parts) % dm.subs

    def part(n):
        return n % dm.parts

    def gpair(n):
        return (n // dm.parts) % 2

    def col(o, xx):
        return al((o * NX + xx) * BLK)

    def w_load(p, w):
        t, u = p // dm.subs, p % dm.subs
        return pltpu.make_async_copy(
            w_hbm.at[t, :, pl.ds(al(w * dm.own + u * BLK), BLK)], wb.at[p % 4, :, pl.ds(w * BLK, BLK)], m_w.at[p % 4, w]
        )

    def xt_load(t):
        return pltpu.make_async_copy(xt_hbm.at[t], xt.at[t], m_ld.at[t])

    def xb_load(t):
        return pltpu.make_async_copy(xm_hbm.at[t], xb, m_ld.at[2])

    def xpb_load(t):
        return pltpu.make_async_copy(xp_hbm.at[t], xpb, m_ld.at[3])

    def x1_copy(n, o):
        return rc(x1_s.at[o], x1_r.at[n % 2, o], m_x1s.at[o], m_x1r.at[n % 2, o], x_dev)

    def xr_copy(n, d, h):
        return rc(xr_s.at[d, h], xr_r.at[n % 2, d, h], m_xrs.at[d, h], m_xrr.at[n % 2, d, h], z_dev(d))

    def zr_copy(n, d, h):
        return rc(zr_s.at[d, h], zr_r.at[n % 2, d, h], m_zrs.at[d, h], m_zrr.at[n % 2, d, h], z_dev(d))

    def z2_copy(n):
        return rc(z2_s, z2_r.at[n % 2], m_z2s, m_z2r.at[n % 2], x_dev)

    def g_x(n, o, xx):
        return gat.at[gpair(n), pl.ds(al(part(n) * rows, 16), rx), pl.ds(col(o, xx), BLK)]

    def g_z(n, o, xx, width):
        return gat.at[gpair(n), pl.ds(al(part(n) * rows + rx, 16), rz), pl.ds(col(o, xx), width)]

    def z4_copy(n):
        return rc(g_z(n, z, x, BLK), g_z(n, z, x, BLK), m_z4s, m_z4r.at[n % 2], x_dev)

    def gx_copy(n, d, h):
        o = z - h if d == 0 else z + h
        return rc(g_x(n, o, x), g_x(n, o, x), m_gxs.at[d, h], m_gxr.at[n % 2, d, h], z_dev(d))

    def gz_copy(n, d, h):
        o = z - h if d == 0 else z + h
        blk = g_z(n, o, 0, NX * BLK)
        return rc(blk, blk, m_gzs.at[d, h], m_gzr.at[n % 2, d, h], z_dev(d))

    def x5_copy(n, o, xx):
        return rc(g_x(n, o, xx), g_x(n, o, xx), m_x5s.at[o], m_x5r.at[n % 2, o], x_dev)

    def c_copy(n, e):
        r = pl.ds(al(part(n) * rows, 16), rows)
        return rc(
            gat.at[gpair(n), r, pl.ds(col(2 * e + 1 - core, 0), NX * BLK)],
            gatp.at[gpair(n), r, pl.ds(e * NX * BLK, NX * BLK)],
            m_cs.at[e], m_cr.at[n % 4, e], c_dev,
        )

    def y_copy(p, q):
        k = pl.ds(q * dm.third, dm.third)
        return rc(y_s.at[k], y_r.at[p % 2, k], m_ys.at[q], m_yr.at[p % 2, q], y_dev)

    def own_copy(p, q, e):
        t, u = p // dm.subs, p % dm.subs
        k = pl.ds(q * dm.third, dm.third)
        return pltpu.make_async_copy(
            own.at[p % 2, k, pl.ds(e * BLK, BLK)],
            wg_hbm.at[t, k, pl.ds(al(e * dm.own + u * BLK), BLK)],
            m_own.at[p % 2, q, e],
        )

    def pg_copy(t, s):
        return pltpu.make_async_copy(pgb, pg_hbm.at[t, :, pl.ds(al(s * rows), rows)], m_pg)

    def sum_copy(k):
        to = lax.rem(bi + k, 4)
        return rc(sum_s.at[to], sum_r.at[k - 1], m_ss.at[k - 1], m_sr.at[k - 1], (wi, to))

    xp_copy = rc(xm_hbm, xp_hbm, m_xps, m_xpr, c_dev)

    def forward(n, k):
        fwd[n % 2, :, pl.ds(k * 256, 256)] = jnp.dot(
            xt[tower(n), pl.ds(al(part(n) * rows, 16), rows), :],
            wb[(n // dm.parts) % 4, :, pl.ds(k * 256, 256)],
            preferred_element_type=F32,
        )

    def x1_send(n, q):
        o = (
            jnp.where(z < 2, 3, 0),
            jnp.where(z < 2, 2, 1),
            jnp.where(z < 2, 1 - z, 5 - z),
            z,
        )[q]

        @pl.when(n >= 1)
        def _():
            x1_copy(n, o).wait_send()

        for r, m in chunks(rx):
            x1_s[o, r : r + m] = fwd[n % 2, r : r + m, pl.ds(col(o, 1 - x), BLK)].astype(BF16)
        x1_copy(n, o).start()

    def xr_hop(n, h):
        for d in (0, 1):
            o = 3 - h + z if d == 0 else h - 3 + z

            @pl.when(far(d) <= h)
            def _():
                x1_copy(n, o).wait_recv()
                if h:
                    @pl.when(far(d) >= 1)
                    def _():
                        xr_copy(n, d, h - 1).wait_recv()

                @pl.when(n >= 1)
                def _():
                    xr_copy(n, d, h).wait_send()

                for r, m in chunks(rx):
                    v = fwd[n % 2, r : r + m, pl.ds(col(o, x), BLK)] + x1_r[n % 2, o, r : r + m].astype(F32)
                    if h:
                        v = v + xr_r[n % 2, d, h - 1, r : r + m].astype(F32)
                    xr_s[d, h, r : r + m] = v.astype(BF16)
                xr_copy(n, d, h).start()

    def zr_hop(n, h):
        for d in (0, 1):
            o = 3 - h + z if d == 0 else h - 3 + z

            @pl.when(far(d) <= h)
            def _():
                if h:
                    @pl.when(far(d) >= 1)
                    def _():
                        zr_copy(n, d, h - 1).wait_recv()

                @pl.when(n >= 1)
                def _():
                    zr_copy(n, d, h).wait_send()

                for r, m in chunks(rz):
                    v = fwd[n % 2, rx + r : rx + r + m, pl.ds(col(o, 0), NX * BLK)]
                    if h:
                        v = v + zr_r[n % 2, d, h - 1, r : r + m].astype(F32)
                    zr_s[d, h, r : r + m] = v.astype(BF16)
                zr_copy(n, d, h).start()

    def z_sum(n):
        for d in (0, 1):
            @pl.when(far(d) >= 1)
            def _():
                zr_copy(n, d, 2).wait_recv()

        @pl.when(n >= 1)
        def _():
            z2_copy(n).wait_send()

        for xx in (1 - x, x):
            for r, m in chunks(rz):
                lanes = pl.ds(al(xx * BLK), BLK)
                v = (
                    fwd[n % 2, rx + r : rx + r + m, pl.ds(col(z, xx), BLK)]
                    + zr_r[n % 2, 0, 2, r : r + m, lanes].astype(F32)
                    + zr_r[n % 2, 1, 2, r : r + m, lanes].astype(F32)
                )
                if xx is x:
                    zown[r : r + m] = v
                else:
                    z2_s[r : r + m] = v.astype(BF16)
            if xx is not x:
                z2_copy(n).start()

    def finish(n, row0, count, total):
        t, u = tower(n), sub(n)
        lanes = pl.ds(al(u * BLK), BLK)
        base = part(n) * rows + row0
        b_row = bias[t, :, lanes]
        from0, from1 = st[t, :, lanes], st[2 + t, :, lanes]
        for r, m in chunks(count):
            at = pl.ds(al(base + r, 16), m)
            v = total(r, m) + b_row
            sq = v * v
            th = jnp.tanh(ROOT * v * (1.0 + CUBE * sq))
            half = 0.5 * (1.0 + th)
            htmp[r : r + m] = v * half
            slope = half + 0.5 * v * (1.0 - th * th) * (ROOT * (1.0 + 3.0 * CUBE * sq))
            up0, up1 = cot[0, at, lanes].astype(F32), cot[1, at, lanes].astype(F32)
            grad = (from0 * up0 + from1 * up1) * slope
            sacc[u, t] += jnp.sum(grad.reshape(m // 8, 8, BLK), axis=0)
            gat[gpair(n), at, pl.ds(col(z, x), BLK)] = grad.astype(BF16)

    def mix(n, row0, count):
        t, u = tower(n), sub(n)
        lanes = pl.ds(al(u * BLK), BLK)
        base = part(n) * rows + row0

        @pl.when(t == 0)
        def _():
            for r, m in chunks(count):
                hid0[pl.ds(al(base + r, 16), m), lanes] = htmp[r : r + m]

        @pl.when(t == 1)
        def _():
            for r, m in chunks(count):
                at = pl.ds(al(base + r, 16), m)
                h = hid0[at, lanes], htmp[r : r + m]
                for i in (0, 1):
                    up = cot[i, at, lanes].astype(F32)
                    out_s[i, at, lanes] = (st[2 * i, :, lanes] * h[0] + st[2 * i + 1, :, lanes] * h[1]).astype(BF16)
                    for j in (0, 1):
                        sacc[u, 2 + 2 * i + j] += jnp.sum((up * h[j]).reshape(m // 8, 8, BLK), axis=0)

    def z_final(n):
        z2_copy(n).wait_recv()
        finish(n, rx, rz, lambda r, m: zown[r : r + m] + z2_r[n % 2, r : r + m].astype(F32))

        @pl.when(n >= 1)
        def _():
            z4_copy(n).wait_send()

        z4_copy(n).start()
        mix(n, rx, rz)

    def x_final(n):
        x1_copy(n, z).wait_recv()
        for d in (0, 1):
            @pl.when(far(d) >= 1)
            def _():
                xr_copy(n, d, 2).wait_recv()

        def total(r, m):
            return (
                fwd[n % 2, r : r + m, pl.ds(col(z, x), BLK)]
                + x1_r[n % 2, z, r : r + m].astype(F32)
                + xr_r[n % 2, 0, 2, r : r + m].astype(F32)
                + xr_r[n % 2, 1, 2, r : r + m].astype(F32)
            )

        finish(n, 0, rx, total)
        for d in (0, 1):
            gather_hop(gx_copy, n, d, 0)
        x5_send(n, z)
        mix(n, 0, rx)

    def gather_hop(copy, n, d, h):
        @pl.when((far(d) >= h) & (far(d) <= 2))
        def _():
            @pl.when(n >= 1)
            def _():
                copy(n, d, h).wait_send()

            copy(n, d, h).start()

    def x5_send(n, o):
        @pl.when(n >= 1)
        def _():
            x5_copy(n, o, x).wait_send()

        x5_copy(n, o, x).start()

    def gather_arrive(copy, n, h, forward_x):
        for d in (0, 1):
            @pl.when(far(d) >= h + 1)
            def _():
                copy(n, d, h).wait_recv()
                if h < 2:
                    gather_hop(copy, n, d, h + 1)
                if forward_x:
                    x5_send(n, z - 1 - h if d == 0 else z + 1 + h)

    def gathered(n):
        for o in range(NZ):
            x5_copy(n, o, 1 - x).wait_recv()
        for e in (0, 1):
            @pl.when(n >= 1)
            def _():
                c_copy(n, e).wait_send()

            c_copy(n, e).start()

    def back_pooled(n):
        t, s = tower(n), part(n)
        lanes = pl.ds(al(s * rows), rows)

        @pl.loop(0, PIECES)
        def _(q):
            k = pl.ds(al(q * dm.third, 16), dm.third)
            acc[k, lanes] += lax.dot_general(
                wb[(n // dm.parts) % 4, k, :],
                gat[gpair(n), pl.ds(al(s * rows, 16), rows), :],
                NT,
                preferred_element_type=F32,
            )

        @pl.when(sub(n) == dm.subs - 1)
        def _():
            @pl.when((t > 0) | (s > 0))
            def _():
                pg_copy(t, s).wait()

            @pl.loop(0, dm.feats // 32)
            def _(k):
                at = pl.ds(al(k * 32, 32), 32)
                pgb[at] = acc[at, lanes].astype(BF16)
                acc[at, lanes] = jnp.zeros((32, rows), F32)

            pg_copy(t, s).start()

    def y_arrive(p, q):
        k = pl.ds(q * dm.third, dm.third)
        y_copy(p, q).wait_recv()
        for r, m in chunks(dm.third):
            at = pl.ds(q * dm.third + r, m)
            own[p % 2, at] += y_r[p % 2, at].astype(F32)
        for e in (0, 1):
            own_copy(p, q, e).start()

    def back_weight(p, q):
        if q == 0:
            for n in (2 * p, 2 * p + 1):
                for e in (0, 1):
                    c_copy(n, e).wait_recv()

            @pl.when(p % dm.subs == 0)
            def _():
                xb_load(p // dm.subs).wait()
                xpb_load(p // dm.subs).wait()

        @pl.when(p >= 1)
        def _():
            y_arrive(p - 1, q)
            y_copy(p, q).wait_send()

        @pl.when(p >= 2)
        def _():
            for e in (0, 1):
                own_copy(p, q, e).wait()

        k = pl.ds(q * dm.third, dm.third)

        def grads(yy):
            lanes = pl.ds(col(2 * yy + core, 0), NX * BLK)
            return jnp.dot(xb[k, :], gat[p % 2, :, lanes], preferred_element_type=F32) + jnp.dot(
                xpb[k, :], gatp[p % 2, :, pl.ds(al(yy * NX * BLK), NX * BLK)], preferred_element_type=F32
            )

        y_s[k, :] = grads(1 - y).astype(BF16)
        y_copy(p, q).start()
        own[p % 2, k, :] = grads(y)

    def sums_send():
        for u in range(dm.subs):
            for j in range(6):
                sum_s[u, j : j + 1] = jnp.sum(sacc[u, j], axis=0, keepdims=True)
            sum_s[u, 6:8] = jnp.zeros((2, BLK), F32)
        for k in (1, 2, 3):
            sum_copy(k).start()

    for w in range(NZ * NX):
        w_load(0, w).start()
    xt_load(0).start()
    for w in range(NZ * NX):
        w_load(1, w).start()
    xt_load(1).start()
    xb_load(0).start()

    barrier = pltpu.get_barrier_semaphore()
    peers = [x_dev] + [(wi, lax.rem(bi + k, 4)) for k in (1, 2, 3)]
    for dev in peers:
        pl.semaphore_signal(barrier, inc=1, device_id=dev, device_id_type=MESH)
    for d in (0, 1):
        @pl.when(far(d) <= 2)
        def _():
            pl.semaphore_signal(barrier, inc=1, device_id=z_dev(d), device_id_type=MESH)

    sacc[...] = jnp.zeros_like(sacc)

    @pl.loop(0, dm.feats // 8)
    def _(k):
        acc[pl.ds(al(k * 8, 8), 8)] = jnp.zeros((8, dm.images), F32)

    for d in (0, 1):
        @pl.when(far(d) == 0)
        def _():
            for s in (0, 1):
                for h in range(3):
                    xr_r[s, d, h] = jnp.zeros((rx, BLK), BF16)
                    zr_r[s, d, h] = jnp.zeros((rz, NX * BLK), BF16)

    pl.semaphore_wait(barrier, jnp.where((z == 0) | (z == NZ - 1), len(peers) + 1, len(peers) + 2))
    xp_copy.start()

    for w in range(NZ * NX):
        w_load(0, w).wait()
    xt_load(0).wait()
    for k in range(4):
        forward(0, k)

    def tick(i, carry):
        a, b, c = i, i - 1, i - 2
        on_a = i < n_units
        on_b = (i >= 1) & (i <= n_units)
        on_c = (i >= 2) & (i <= n_units + 1)
        on_f = i + 1 < n_units
        p = lax.div(i - 4, 2)
        on_p = (i >= 4) & (i % 2 == 0)

        @pl.when(on_a)
        def _():
            x1_send(a, 0)
            zr_hop(a, 0)

        @pl.when((i % 2 == 0) & (i // 2 + 2 < dm.towers * dm.subs))
        def _():
            for w in range(NZ * NX):
                w_load(i // 2 + 2, w).start()

        @pl.when(on_b)
        def _():
            z_final(b)
            x_final(b)

        @pl.when(on_c)
        def _():
            gather_arrive(gz_copy, c, 0, False)

        @pl.when(on_f)
        def _():
            @pl.when(i % 2 == 1)
            def _():
                for w in range(NZ * NX):
                    w_load((i + 1) // 2, w).wait()

            @pl.when(i + 1 == n_units // 2)
            def _():
                xt_load(1).wait()

            forward(i + 1, 0)

        @pl.when(on_p)
        def _():
            back_weight(p, 0)

        @pl.when(on_a)
        def _():
            x1_send(a, 1)
            zr_hop(a, 1)
            xr_hop(a, 0)

        @pl.when(on_c)
        def _():
            gather_arrive(gz_copy, c, 1, False)

        @pl.when(on_b)
        def _():
            gather_arrive(gx_copy, b, 0, True)

        @pl.when(on_f)
        def _():
            forward(i + 1, 1)

        @pl.when(on_p)
        def _():
            back_weight(p, 1)

        @pl.when(on_a)
        def _():
            x1_send(a, 2)
            zr_hop(a, 2)
            xr_hop(a, 1)

        @pl.when(on_b)
        def _():
            gather_arrive(gx_copy, b, 1, True)

        @pl.when(on_c)
        def _():
            gather_arrive(gz_copy, c, 2, False)
            gathered(c)

        @pl.when(on_f)
        def _():
            forward(i + 1, 2)

        @pl.when(on_p)
        def _():
            back_weight(p, 2)

        @pl.when(on_a)
        def _():
            x1_send(a, 3)
            z_sum(a)
            xr_hop(a, 2)

        @pl.when(on_b)
        def _():
            z4_copy(b).wait_recv()
            for d in (0, 1):
                gather_hop(gz_copy, b, d, 0)
            gather_arrive(gx_copy, b, 2, True)

        @pl.when(on_c)
        def _():
            back_pooled(c)

        @pl.when(on_f)
        def _():
            forward(i + 1, 3)

        @pl.when(i == 3)
        def _():
            xp_copy.wait_recv()
            xpb_load(0).start()

        @pl.when(i == 2 * dm.subs + 3)
        def _():
            xb_load(1).start()
            xpb_load(1).start()

        @pl.when(i == n_units)
        def _():
            sums_send()

        return carry

    lax.fori_loop(0, n_units + 3, tick, 0)

    last, pairs = n_units - 1, dm.towers * dm.subs
    for k in (1, 2, 3):
        sum_copy(k).wait_recv()
    total = sum_s[bi] + sum_r[0] + sum_r[1] + sum_r[2]
    out_small[0] = total
    out_small[1] = st8[:, pl.ds(al(bi * BLK), BLK)] - step_ref[0] * total
    for q in range(PIECES):
        y_arrive(pairs - 1, q)
    for q in range(PIECES):
        for e in (0, 1):
            own_copy(pairs - 2, q, e).wait()
            own_copy(pairs - 1, q, e).wait()
        y_copy(pairs - 1, q).wait_send()
    pg_copy(1, 1).wait()
    xp_copy.wait_send()
    for k in (1, 2, 3):
        sum_copy(k).wait_send()
    for e in (0, 1):
        c_copy(last, e).wait_send()
    for o in range(NZ):
        x1_copy(last, o).wait_send()
        x5_copy(last, o, x).wait_send()
    z2_copy(last).wait_send()
    z4_copy(last).wait_send()
    for d in (0, 1):
        for h in range(3):
            @pl.when(far(d) <= h)
            def _():
                xr_copy(last, d, h).wait_send()
                zr_copy(last, d, h).wait_send()

            @pl.when((far(d) >= h) & (far(d) <= 2))
            def _():
                gx_copy(last, d, h).wait_send()
                gz_copy(last, d, h).wait_send()


def fused(pooled, weight, fc_bias, stitch, cotangent, factor, step_rate):
    dm = Dims(pooled, weight, cotangent)
    masked = pooled * factor[None]
    masked_t = jnp.swapaxes(masked, 1, 2)
    cot_t = jnp.swapaxes(cotangent, 1, 2)
    towers, feats, images, own = dm.towers, dm.feats, dm.images, dm.own
    rows, rx, rz, cols = dm.rows, dm.rx, dm.rz, dm.cols
    dma = pltpu.SemaphoreType.DMA
    vm = pltpu.VMEM
    scratch = [
        vm((4, feats, cols), BF16),
        vm((towers, images, feats), BF16),
        vm((feats, images), BF16),
        vm((feats, images), BF16),
        vm((feats, images), F32),
        vm((2, rows, cols), F32),
        vm((2, images, cols), BF16),
        vm((2, images, cols // 2), BF16),
        vm((NZ, rx, BLK), BF16),
        vm((2, NZ, rx, BLK), BF16),
        vm((2, 3, rx, BLK), BF16),
        vm((2, 2, 3, rx, BLK), BF16),
        vm((2, 3, rz, NX * BLK), BF16),
        vm((2, 2, 3, rz, NX * BLK), BF16),
        vm((rz, BLK), F32),
        vm((rz, BLK), BF16),
        vm((2, rz, BLK), BF16),
        vm((2, feats, NX * BLK), F32),
        vm((feats, NX * BLK), BF16),
        vm((2, feats, NX * BLK), BF16),
        vm((images, own), F32),
        vm((max(rx, rz), BLK), F32),
        vm((feats, rows), BF16),
        vm((dm.subs, 6, 8, BLK), F32),
        vm((dm.subs, 8, BLK), F32),
        vm((3, 8, BLK), F32),
    ] + [
        dma(shape)
        for shape in (
            (4, NZ * NX), (4,), (NZ,), (2, NZ), (2, 3), (2, 2, 3), (2, 3), (2, 2, 3), (), (2,), (), (2,),
            (2, 3), (2, 2, 3), (2, 3), (2, 2, 3), (NZ,), (2, NZ), (2,), (4, 2), (PIECES,), (2, PIECES), (3,), (3,), (), (),
            (2, PIECES, 2), (),
        )
    ]
    anyspace = pl.BlockSpec(memory_space=pl.ANY)
    inside = pl.BlockSpec(memory_space=pltpu.VMEM)
    st8 = jnp.pad(stitch.reshape(4, own), ((2, 2), (0, 0)))
    stitched_t, pooled_raw, weight_grad, small, _ = pl.pallas_call(
        functools.partial(kernel, dm),
        name="stitch_fc6",
        out_shape=[
            jax.ShapeDtypeStruct((2, images, own), BF16),
            jax.ShapeDtypeStruct((towers, feats, images), BF16),
            jax.ShapeDtypeStruct((towers, feats, images), F32),
            jax.ShapeDtypeStruct((2, 8, BLK), F32),
            jax.ShapeDtypeStruct((towers, feats, images), BF16),
        ],
        in_specs=[pl.BlockSpec(memory_space=pltpu.SMEM), anyspace, anyspace, anyspace, inside, inside, inside, inside],
        out_specs=[inside, anyspace, anyspace, inside, anyspace],
        scratch_shapes=scratch,
        compiler_params=pltpu.CompilerParams(collective_id=1, has_side_effects=True, vmem_limit_bytes=60 * 2**20),
        cost_estimate=pl.CostEstimate(
            flops=6 * towers * feats * images * dm.chans, bytes_accessed=60 * 2**20, transcendentals=towers * images * own
        ),
    )(
        step_rate, weight, masked, masked_t, cot_t,
        fc_bias.reshape(towers, 1, own), stitch.reshape(4, 1, own), st8,
    )
    stitched = jnp.swapaxes(stitched_t, 1, 2)
    pooled_grad = pooled_raw * factor[None]
    sums, moved = small[0], small[1]
    return (
        stitched,
        pooled_grad,
        weight_grad,
        sums[:2],
        sums[2:6].reshape(2, 2, BLK),
        moved[2:6].reshape(2, 2, BLK),
    )


def gelu_local(values):
    return jax.nn.gelu(values, approximate=True)


def plain(pooled, weight, fc_bias, stitch, cotangent, factor, step_rate):
    highest = lax.Precision.HIGHEST
    masked = pooled * factor[None]
    owned = weight.shape[2] // lax.axis_size("wide")
    summed = lax.psum_scatter(
        jnp.einsum("tkc,tkb->ctb", weight, masked, preferred_element_type=F32), "wide", scatter_dimension=0, tiled=True
    )
    pre_act = summed + jnp.transpose(fc_bias)[:, :, None]
    hidden, gelu_back = jax.vjp(gelu_local, pre_act)
    stitched = jnp.einsum("ijc,cjb->icb", stitch, hidden, precision=highest)
    upstream = cotangent.astype(F32)
    stitch_part = jnp.einsum("icb,cjb->ijc", upstream, hidden, precision=highest)
    hidden_grad = jnp.einsum("ijc,icb->cjb", stitch, upstream, precision=highest)
    pre_grad = gelu_back(hidden_grad)[0]
    bias_part = jnp.transpose(jnp.sum(pre_grad, axis=2))
    pre_low = pre_grad.astype(BF16)
    bias_grad = lax.psum_scatter(bias_part, "batch", scatter_dimension=1, tiled=True)
    stitch_grad = lax.psum_scatter(stitch_part, "batch", scatter_dimension=2, tiled=True)
    portion = lax.all_gather(pre_low, "wide", axis=0, tiled=True)
    input_sum = jnp.einsum("tkc,ctb->tkb", weight, portion, preferred_element_type=F32)
    block_grad = jnp.einsum("tkb,ctb->tkc", masked, portion, preferred_element_type=F32)
    pooled_grad = (input_sum * factor.astype(F32)[None]).astype(BF16)
    weight_grad = lax.psum_scatter(block_grad, "batch", scatter_dimension=2, tiled=True)
    share = owned // lax.axis_size("batch")
    stitch_mine = lax.dynamic_slice_in_dim(stitch, lax.axis_index("batch") * share, share, 2)
    stitch_new = stitch_mine - step_rate[0] * stitch_grad
    return stitched.astype(BF16), pooled_grad, weight_grad, bias_grad, stitch_grad, stitch_new


def fits(mesh, pooled, weight, cotangent):
    return (
        (mesh.shape["wide"], mesh.shape["batch"]) == (NZ * NX, 4)
        and pooled.shape[0] == 2
        and cotangent.shape[1] == 4 * BLK
        and weight.shape[2] == NZ * NX * cotangent.shape[1]
        and pooled.shape[2] % 512 == 0
        and pooled.shape[1] % (16 * PIECES) == 0
    )


def solution(mesh):
    def body(pooled, weight, fc_bias, stitch, cotangent, valid_mask, image_group, step_rate):
        factor = 1.0 - image_group[None, :].astype(F32) * (1.0 - valid_mask[:, None].astype(F32))
        form = fused if fits(mesh, pooled, weight, cotangent) else plain
        return form(pooled, weight, fc_bias, stitch, cotangent, factor.astype(BF16), step_rate)

    return jax.shard_map(
        body,
        mesh=mesh,
        in_specs=(
            P(None, "wide", "batch"),
            P(None, "wide", None),
            P(None, "wide"),
            P(None, None, "wide"),
            P(None, "wide", "batch"),
            P("wide"),
            P("batch"),
            P(),
        ),
        out_specs=(
            P(None, "wide", "batch"),
            P(None, "wide", "batch"),
            P(None, "wide", "batch"),
            P(None, ("wide", "batch")),
            P(None, None, ("wide", "batch")),
            P(None, None, ("wide", "batch")),
        ),
        check_vma=False,
    )
```

time: 1130 us -> 423 us (0.37)
  waiting for transfers between devices: 907 us -> 0 us
  Pallas kernels: 0 us -> 355 us
  matrix products: 134 us -> 0 us
  blocking collectives: 24.3 us -> 0 us
  local copies, waits for them, and re-layouts: 34.5 us -> 50.1 us
  between operations: 15.4 us -> 1.31 us
    reduce_scatter x2 -> x0, waiting for transfers between devices: 681 us -> none  [the longest x1 528 us: body(): lax.psum_scatter(jnp.einsum('tkc,tkb->ctb', picked, masked, preferred_ele...]
    pallas_call x0 -> x1, Pallas kernels: none -> 355 us  [fused(): pl.pallas_call(functools.partial(kernel, dm), name='stitch_fc6', out_shap...]
    all_gather x1 -> x0, waiting for transfers between devices: 226 us -> none  [body(): portion = lax.all_gather(pre_low, 'wide', axis=0, tiled=True)]
    dot_general x6 -> x0, matrix products: 134 us -> none  [the longest x1 31.3 us: body(): jnp.einsum('tkc,ctb->tkb', picked, portion, preferred_element_type=jnp.fl...]
    unnamed x1 -> x0, blocking collectives: 24.3 us -> none
    unnamed x18 -> x7, local copies, waits for them, and re-layouts: 15.2 us -> 30.5 us
  transfers between devices with their start and end apart: 4 -> 0, of which waited for: 3 -> 0; matrix products, arithmetic and copies ran while one was open for 12% -> 0% of each run, Pallas kernels for 0% -> 0%
where the time goes in v1:
time: 423 us; the launch traced here: 422 us
  Pallas kernels  355 us (84%)
  local copies, waits for them, and re-layouts  50.1 us (12%)
  other arithmetic  15 us (4%)
    pallas_call x1, Pallas kernels, fused(): pl.pallas_call(functools.partial(kernel, dm), name='stitch_fc6', out_shap...  355 us
    unnamed x7, local copies, waits for them, and re-layouts  30.5 us

profile of v1, /device:TPU:0, one launch (start us, length us, event | category | flops | bytes accessed | tf_op | source)
XLA Modules:
  0.0 421.7 jit_solution(12870219429781533628)
XLA Ops:
  1.3 1.3 reshape.64.bias
  2.6 0.7 convert_element_type.17
  3.2 0.7 convert_subtract_fusion
  3.9 0.7 reshape.66
  4.7 0.6 pad.4.st8
  5.3 1.3 reshape.65.st
  6.6 3.9 copy.15
  10.5 0.5 subtract_convert_fusion
  11.0 6.6 %copy.14 = bf16[2,1152,1024]{1,2,0:T(8,128)(2,1)} copy(bf16[2,1152,1024]{2,1,0:T(8,128)(2,1)} %param.8) | data formatting | bytes 9437184 | tf_op args[0]
  17.6 0.0 copy-start
  17.6 5.2 %fusion.1.xt_hbm = bf16[2,1024,1152]{2,1,0:T(8,128)(2,1)} fusion(bf16[2,1152,1024]{1,2,0:T(8,128)(2,1)} %copy.14, bf16[1152,1024]{0,1:T(8,128)(2,1)S(1)} %subtract_convert_fusion), kind=kLoop, calls=%fused_computation.6 | loop fusion | flops 2359296 | bytes 11796480 | tf_op jit(solution)/shard_map/transpose | solution.py:651
  22.9 0.0 copy-done
  22.9 2.9 broadcast_multiply_fusion.1
  25.7 6.6 %copy.16.xm_hbm = bf16[2,1152,1024]{2,1,0:T(8,128)(2,1)} copy(bf16[2,1152,1024]{1,2,0:T(8,128)(2,1)} %broadcast_multiply_fusion.1) | data formatting | bytes 9437184 | tf_op jit(solution)/shard_map/mul | solution.py:650
  32.3 355.4 %stitch_fc6.1 = (bf16[2,1024,512]{2,1,0:T(8,128)(2,1)}, bf16[2,1152,1024]{2,1,0:T(8,128)(2,1)}, f32[2,1152,1024]{2,1,0:T(8,128)}, f32[2,8,128]{2,1,0:T(8,128)}, bf16[2,1152,1024]{2,1,0:T(8,128)(2,1)}) custom-call(f32[1]{0:T(128)S(6)} %copy.21.step_ref, bf16[2,1152,4096]{2,1,0:T(8,128)(2,1)} %w_hbm.1, bf16[2,1152,1024]{2,1,0:T(8,128)(2,1)} %copy.16.xm_hbm, ...), custom_call_target="tpu_custom_call" | custom-call | flops 57982058496 | bytes 62914560 | tf_op jit(solution)/shard_map/stitch_fc6/pallas_call | solution.py:695
  387.7 3.9 copy.18
  391.6 1.2 slice_bitcast_fusion
  392.9 1.3 fusion
  394.1 6.6 %copy.17 = bf16[2,1152,1024]{1,2,0:T(8,128)(2,1)} copy(bf16[2,1152,1024]{2,1,0:T(8,128)(2,1)} %get-tuple-element.11) | data formatting | bytes 9437184 | tf_op jit(solution)/shard_map/stitch_fc6/pallas_call | solution.py:695
  400.7 5.0 %broadcast_multiply_fusion = bf16[2,1152,1024]{1,2,0:T(8,128)(2,1)} fusion(bf16[2,1152,1024]{1,2,0:T(8,128)(2,1)} %copy.17, bf16[1152,1024]{0,1:T(8,128)(2,1)S(1)} %subtract_convert_fusion), kind=kLoop, calls=%fused_computation.1 | loop fusion | flops 2359296 | bytes 11796480 | tf_op jit(solution)/shard_map/mul | solution.py:717
  405.8 6.6 %copy.19 = bf16[2,1152,1024]{2,1,0:T(8,128)(2,1)} copy(bf16[2,1152,1024]{1,2,0:T(8,128)(2,1)} %broadcast_multiply_fusion) | data formatting | bytes 9437184
  412.4 9.4 %copy.22 = f32[2,1152,1024]{2,1,0:T(8,128)} copy(f32[2,1152,1024]{2,1,0:T(8,128)} %get-tuple-element.30) | data formatting | bytes 18874368
Async XLA Ops:
  17.6 5.2 %copy-start = (bf16[2,1152,1024]{1,2,0:T(8,128)(2,1)S(1)}, bf16[2,1152,1024]{1,2,0:T(8,128)(2,1)}, u32[]{:S(2)}) copy-start(bf16[2,1152,1024]{1,2,0:T(8,128)(2,1)} %copy.14) | copy-start | bytes 14155780

commit v2 on v1

--- a/solution.py
+++ b/solution.py
@@ -16,6 +16,7 @@
 ROOT = math.sqrt(2.0 / math.pi)
 CUBE = 0.044715
 PIECES = 3
+CUTS = 4
 
 
 class Dims:
@@ -39,13 +40,14 @@
 
 def kernel(
     dm,
-    step_ref, w_hbm, xm_hbm, xt_hbm, cot, bias, st, st8,
-    out_s, pg_hbm, wg_hbm, out_small, xp_hbm,
-    wb, xt, xb, xpb, acc, fwd, gat, gatp,
+    step_ref, w_hbm, p_hbm, c_hbm, bias, st, valid, group,
+    s_hbm, pg_hbm, wg_hbm, out_b, out_sg, out_sn,
+    wb, xt, xb, xpb, hole, small_img, craw, cot, stmp, sbuf, acc, fwd, gat, gatp,
     x1_s, x1_r, xr_s, xr_r, zr_s, zr_r, zown, z2_s, z2_r,
     own, y_s, y_r, hid0, htmp, pgb, sacc, sum_s, sum_r,
     m_w, m_ld, m_x1s, m_x1r, m_xrs, m_xrr, m_zrs, m_zrr, m_z2s, m_z2r, m_z4s, m_z4r,
     m_gxs, m_gxr, m_gzs, m_gzr, m_x5s, m_x5r, m_cs, m_cr, m_ys, m_yr, m_ss, m_sr, m_xps, m_xpr, m_own, m_pg,
+    m_cot, m_out,
 ):
     n_units, rows, rx, rz = dm.units, dm.rows, dm.rx, dm.rz
     wi, bi = lax.axis_index("wide"), lax.axis_index("batch")
@@ -88,14 +90,22 @@
             w_hbm.at[t, :, pl.ds(al(w * dm.own + u * BLK), BLK)], wb.at[p % 4, :, pl.ds(w * BLK, BLK)], m_w.at[p % 4, w]
         )
 
-    def xt_load(t):
-        return pltpu.make_async_copy(xt_hbm.at[t], xt.at[t], m_ld.at[t])
-
-    def xb_load(t):
-        return pltpu.make_async_copy(xm_hbm.at[t], xb, m_ld.at[2])
-
-    def xpb_load(t):
-        return pltpu.make_async_copy(xp_hbm.at[t], xpb, m_ld.at[3])
+    def x_load(t, s):
+        lanes = pl.ds(s * rows, rows)
+        return pltpu.make_async_copy(p_hbm.at[t, :, lanes], xb.at[t, :, lanes], m_ld.at[t, s])
+
+    def cot_load(n, i):
+        return pltpu.make_async_copy(
+            c_hbm.at[i, pl.ds(al(sub(n) * BLK), BLK), pl.ds(al(part(n) * rows), rows)], craw.at[n % 2, i], m_cot.at[n % 2, i]
+        )
+
+    def s_copy(n, i):
+        return pltpu.make_async_copy(
+            sbuf.at[n % 2, i], s_hbm.at[i, pl.ds(al(sub(n) * BLK), BLK), pl.ds(al(part(n) * rows), rows)], m_out.at[n % 2, i]
+        )
+
+    def xp_copy(t):
+        return rc(xb.at[t], xpb.at[t], m_xps.at[t], m_xpr.at[t], c_dev)
 
     def x1_copy(n, o):
         return rc(x1_s.at[o], x1_r.at[n % 2, o], m_x1s.at[o], m_x1r.at[n % 2, o], x_dev)
@@ -158,7 +168,22 @@
         to = lax.rem(bi + k, 4)
         return rc(sum_s.at[to], sum_r.at[k - 1], m_ss.at[k - 1], m_sr.at[k - 1], (wi, to))
 
-    xp_copy = rc(xm_hbm, xp_hbm, m_xps, m_xpr, c_dev)
+    def factor(k, s):
+        wide_hole = jnp.concatenate([hole[pl.ds(al(k * BLK), BLK)]] * (rows // BLK), axis=1)
+        return 1.0 - small_img[:, pl.ds(al(s * rows), rows)] * wide_hole
+
+    def prepare(t, s):
+        @pl.loop(0, dm.feats // BLK)
+        def _(k):
+            at, lanes = pl.ds(al(k * BLK), BLK), pl.ds(s * rows, rows)
+            masked = (xb[t, at, lanes].astype(F32) * factor(k, s)).astype(BF16)
+            xb[t, at, lanes] = masked
+            xt[t, pl.ds(s * rows, rows), at] = masked.T
+
+    def prepare_cot(n):
+        for i in (0, 1):
+            cot_load(n, i).wait()
+            cot[i, pl.ds(al(part(n) * rows), rows), pl.ds(al(sub(n) * BLK), BLK)] = craw[n % 2, i].T
 
     def forward(n, k):
         fwd[n % 2, :, pl.ds(k * 256, 256)] = jnp.dot(
@@ -257,8 +282,9 @@
         t, u = tower(n), sub(n)
         lanes = pl.ds(al(u * BLK), BLK)
         base = part(n) * rows + row0
-        b_row = bias[t, :, lanes]
-        from0, from1 = st[t, :, lanes], st[2 + t, :, lanes]
+        b_row = jnp.where(t == 0, bias[0:1, lanes], bias[1:2, lanes])
+        from0 = jnp.where(t == 0, st[0, 0:1, lanes], st[0, 1:2, lanes])
+        from1 = jnp.where(t == 0, st[1, 0:1, lanes], st[1, 1:2, lanes])
         for r, m in chunks(count):
             at = pl.ds(al(base + r, 16), m)
             v = total(r, m) + b_row
@@ -289,9 +315,20 @@
                 h = hid0[at, lanes], htmp[r : r + m]
                 for i in (0, 1):
                     up = cot[i, at, lanes].astype(F32)
-                    out_s[i, at, lanes] = (st[2 * i, :, lanes] * h[0] + st[2 * i + 1, :, lanes] * h[1]).astype(BF16)
+                    stmp[i, row0 + r : row0 + r + m] = (st[i, 0:1, lanes] * h[0] + st[i, 1:2, lanes] * h[1]).astype(BF16)
                     for j in (0, 1):
                         sacc[u, 2 + 2 * i + j] += jnp.sum((up * h[j]).reshape(m // 8, 8, BLK), axis=0)
+
+    def emit(n):
+        @pl.when(tower(n) == 1)
+        def _():
+            for i in (0, 1):
+                @pl.when(n >= n_units // 2 + 2)
+                def _():
+                    s_copy(n, i).wait()
+
+                sbuf[n % 2, i] = stmp[i].T
+                s_copy(n, i).start()
 
     def z_final(n):
         z2_copy(n).wait_recv()
@@ -381,11 +418,11 @@
             def _():
                 pg_copy(t, s).wait()
 
-            @pl.loop(0, dm.feats // 32)
+            @pl.loop(0, dm.feats // BLK)
             def _(k):
-                at = pl.ds(al(k * 32, 32), 32)
-                pgb[at] = acc[at, lanes].astype(BF16)
-                acc[at, lanes] = jnp.zeros((32, rows), F32)
+                at = pl.ds(al(k * BLK), BLK)
+                pgb[at] = (acc[at, lanes] * factor(k, s)).astype(BF16)
+                acc[at, lanes] = jnp.zeros((BLK, rows), F32)
 
             pg_copy(t, s).start()
 
@@ -406,8 +443,7 @@
 
             @pl.when(p % dm.subs == 0)
             def _():
-                xb_load(p // dm.subs).wait()
-                xpb_load(p // dm.subs).wait()
+                xp_copy(p // dm.subs).wait_recv()
 
         @pl.when(p >= 1)
         def _():
@@ -419,12 +455,12 @@
             for e in (0, 1):
                 own_copy(p, q, e).wait()
 
-        k = pl.ds(q * dm.third, dm.third)
+        t, k = p // dm.subs, pl.ds(q * dm.third, dm.third)
 
         def grads(yy):
             lanes = pl.ds(col(2 * yy + core, 0), NX * BLK)
-            return jnp.dot(xb[k, :], gat[p % 2, :, lanes], preferred_element_type=F32) + jnp.dot(
-                xpb[k, :], gatp[p % 2, :, pl.ds(al(yy * NX * BLK), NX * BLK)], preferred_element_type=F32
+            return jnp.dot(xb[t, k, :], gat[p % 2, :, lanes], preferred_element_type=F32) + jnp.dot(
+                xpb[t, k, :], gatp[p % 2, :, pl.ds(al(yy * NX * BLK), NX * BLK)], preferred_element_type=F32
             )
 
         y_s[k, :] = grads(1 - y).astype(BF16)
@@ -439,13 +475,16 @@
         for k in (1, 2, 3):
             sum_copy(k).start()
 
+    x_load(0, 0).start()
     for w in range(NZ * NX):
         w_load(0, w).start()
-    xt_load(0).start()
+    x_load(0, 1).start()
+    for i in (0, 1):
+        cot_load(0, i).start()
     for w in range(NZ * NX):
         w_load(1, w).start()
-    xt_load(1).start()
-    xb_load(0).start()
+    for s in (0, 1):
+        x_load(1, s).start()
 
     barrier = pltpu.get_barrier_semaphore()
     peers = [x_dev] + [(wi, lax.rem(bi + k, 4)) for k in (1, 2, 3)]
@@ -456,7 +495,12 @@
         def _():
             pl.semaphore_signal(barrier, inc=1, device_id=z_dev(d), device_id_type=MESH)
 
-    sacc[...] = jnp.zeros_like(sacc)
+    small_img[...] = jnp.concatenate([group[j : j + 1] for j in range(dm.images // BLK)], axis=1).astype(F32)
+    for j in range(dm.feats // BLK):
+        gap = 1.0 - valid[j : j + 1].astype(F32)
+        hole[j * BLK : (j + 1) * BLK] = jnp.broadcast_to(gap, (BLK, BLK)).T
+    x_load(0, 0).wait()
+    prepare(0, 0)
 
     @pl.loop(0, dm.feats // 8)
     def _(k):
@@ -471,13 +515,11 @@
                     zr_r[s, d, h] = jnp.zeros((rz, NX * BLK), BF16)
 
     pl.semaphore_wait(barrier, jnp.where((z == 0) | (z == NZ - 1), len(peers) + 1, len(peers) + 2))
-    xp_copy.start()
-
     for w in range(NZ * NX):
         w_load(0, w).wait()
-    xt_load(0).wait()
     for k in range(4):
         forward(0, k)
+    sacc[...] = jnp.zeros_like(sacc)
 
     def tick(i, carry):
         a, b, c = i, i - 1, i - 2
@@ -514,9 +556,11 @@
                 for w in range(NZ * NX):
                     w_load((i + 1) // 2, w).wait()
 
-            @pl.when(i + 1 == n_units // 2)
-            def _():
-                xt_load(1).wait()
+            @pl.when(i == 0)
+            def _():
+                x_load(0, 1).wait()
+                prepare(0, 1)
+                xp_copy(0).start()
 
             forward(i + 1, 0)
 
@@ -537,6 +581,7 @@
         @pl.when(on_b)
         def _():
             gather_arrive(gx_copy, b, 0, True)
+            emit(b)
 
         @pl.when(on_f)
         def _():
@@ -560,6 +605,15 @@
         def _():
             gather_arrive(gz_copy, c, 2, False)
             gathered(c)
+
+        @pl.when(i < n_units // 2)
+        def _():
+            prepare_cot(i)
+
+            @pl.when(i + 1 < n_units // 2)
+            def _():
+                for j in (0, 1):
+                    cot_load(i + 1, j).start()
 
         @pl.when(on_f)
         def _():
@@ -590,15 +644,13 @@
         def _():
             forward(i + 1, 3)
 
-        @pl.when(i == 3)
-        def _():
-            xp_copy.wait_recv()
-            xpb_load(0).start()
-
-        @pl.when(i == 2 * dm.subs + 3)
-        def _():
-            xb_load(1).start()
-            xpb_load(1).start()
+        for s in (0, 1):
+            @pl.when(i == 4 + s)
+            def _():
+                x_load(1, s).wait()
+                prepare(1, s)
+                if s:
+                    xp_copy(1).start()
 
         @pl.when(i == n_units)
         def _():
@@ -612,8 +664,10 @@
     for k in (1, 2, 3):
         sum_copy(k).wait_recv()
     total = sum_s[bi] + sum_r[0] + sum_r[1] + sum_r[2]
-    out_small[0] = total
-    out_small[1] = st8[:, pl.ds(al(bi * BLK), BLK)] - step_ref[0] * total
+    out_b[...] = total[0:2]
+    for i in (0, 1):
+        out_sg[i] = total[2 + 2 * i : 4 + 2 * i]
+        out_sn[i] = st[i, :, pl.ds(al(bi * BLK), BLK)] - step_ref[0] * total[2 + 2 * i : 4 + 2 * i]
     for q in range(PIECES):
         y_arrive(pairs - 1, q)
     for q in range(PIECES):
@@ -622,7 +676,11 @@
             own_copy(pairs - 1, q, e).wait()
         y_copy(pairs - 1, q).wait_send()
     pg_copy(1, 1).wait()
-    xp_copy.wait_send()
+    for i in (0, 1):
+        s_copy(last - 1, i).wait()
+        s_copy(last, i).wait()
+    for t in range(dm.towers):
+        xp_copy(t).wait_send()
     for k in (1, 2, 3):
         sum_copy(k).wait_send()
     for e in (0, 1):
@@ -645,11 +703,14 @@
                 gz_copy(last, d, h).wait_send()
 
 
-def fused(pooled, weight, fc_bias, stitch, cotangent, factor, step_rate):
+def carry_out(*refs):
+    count = len(refs) // 2
+    for src, dst in zip(refs[:count], refs[count:]):
+        dst[...] = src[...]
+
+
+def fused(pooled, weight, fc_bias, stitch, cotangent, valid_mask, image_group, step_rate):
     dm = Dims(pooled, weight, cotangent)
-    masked = pooled * factor[None]
-    masked_t = jnp.swapaxes(masked, 1, 2)
-    cot_t = jnp.swapaxes(cotangent, 1, 2)
     towers, feats, images, own = dm.towers, dm.feats, dm.images, dm.own
     rows, rx, rz, cols = dm.rows, dm.rx, dm.rz, dm.cols
     dma = pltpu.SemaphoreType.DMA
@@ -657,8 +718,14 @@
     scratch = [
         vm((4, feats, cols), BF16),
         vm((towers, images, feats), BF16),
-        vm((feats, images), BF16),
-        vm((feats, images), BF16),
+        vm((towers, feats, images), BF16),
+        vm((towers, feats, images), BF16),
+        vm((feats, BLK), F32),
+        vm((1, images), F32),
+        vm((2, 2, BLK, rows), BF16),
+        vm((2, images, own), BF16),
+        vm((2, rows, BLK), BF16),
+        vm((2, 2, BLK, rows), BF16),
         vm((feats, images), F32),
         vm((2, rows, cols), F32),
         vm((2, images, cols), BF16),
@@ -684,55 +751,62 @@
     ] + [
         dma(shape)
         for shape in (
-            (4, NZ * NX), (4,), (NZ,), (2, NZ), (2, 3), (2, 2, 3), (2, 3), (2, 2, 3), (), (2,), (), (2,),
-            (2, 3), (2, 2, 3), (2, 3), (2, 2, 3), (NZ,), (2, NZ), (2,), (4, 2), (PIECES,), (2, PIECES), (3,), (3,), (), (),
-            (2, PIECES, 2), (),
+            (4, NZ * NX), (2, 2), (NZ,), (2, NZ), (2, 3), (2, 2, 3), (2, 3), (2, 2, 3), (), (2,), (), (2,),
+            (2, 3), (2, 2, 3), (2, 3), (2, 2, 3), (NZ,), (2, NZ), (2,), (4, 2), (PIECES,), (2, PIECES), (3,), (3,), (2,), (2,),
+            (2, PIECES, 2), (), (2, 2), (2, 2),
         )
     ]
     anyspace = pl.BlockSpec(memory_space=pl.ANY)
     inside = pl.BlockSpec(memory_space=pltpu.VMEM)
-    st8 = jnp.pad(stitch.reshape(4, own), ((2, 2), (0, 0)))
-    stitched_t, pooled_raw, weight_grad, small, _ = pl.pallas_call(
+    out_shape = [
+        jax.ShapeDtypeStruct((2, own, images), BF16),
+        jax.ShapeDtypeStruct((towers, feats, images), BF16),
+        jax.ShapeDtypeStruct((towers, feats, images), F32),
+        jax.ShapeDtypeStruct((2, BLK), F32),
+        jax.ShapeDtypeStruct((2, 2, BLK), F32),
+        jax.ShapeDtypeStruct((2, 2, BLK), F32),
+    ]
+    out_specs = [anyspace] * 3 + [inside] * 3
+    results = pl.pallas_call(
         functools.partial(kernel, dm),
         name="stitch_fc6",
-        out_shape=[
-            jax.ShapeDtypeStruct((2, images, own), BF16),
-            jax.ShapeDtypeStruct((towers, feats, images), BF16),
-            jax.ShapeDtypeStruct((towers, feats, images), F32),
-            jax.ShapeDtypeStruct((2, 8, BLK), F32),
-            jax.ShapeDtypeStruct((towers, feats, images), BF16),
-        ],
-        in_specs=[pl.BlockSpec(memory_space=pltpu.SMEM), anyspace, anyspace, anyspace, inside, inside, inside, inside],
-        out_specs=[inside, anyspace, anyspace, inside, anyspace],
+        out_shape=out_shape,
+        in_specs=[pl.BlockSpec(memory_space=pltpu.SMEM)] + [anyspace] * 3 + [inside] * 4,
+        out_specs=out_specs,
         scratch_shapes=scratch,
-        compiler_params=pltpu.CompilerParams(collective_id=1, has_side_effects=True, vmem_limit_bytes=60 * 2**20),
+        compiler_params=pltpu.CompilerParams(collective_id=1, has_side_effects=True, vmem_limit_bytes=61 * 2**20),
         cost_estimate=pl.CostEstimate(
             flops=6 * towers * feats * images * dm.chans, bytes_accessed=60 * 2**20, transcendentals=towers * images * own
         ),
     )(
-        step_rate, weight, masked, masked_t, cot_t,
-        fc_bias.reshape(towers, 1, own), stitch.reshape(4, 1, own), st8,
+        step_rate, weight, pooled, cotangent, fc_bias, stitch,
+        valid_mask.reshape(feats // BLK, BLK), image_group.reshape(images // BLK, BLK),
     )
-    stitched = jnp.swapaxes(stitched_t, 1, 2)
-    pooled_grad = pooled_raw * factor[None]
-    sums, moved = small[0], small[1]
-    return (
-        stitched,
-        pooled_grad,
-        weight_grad,
-        sums[:2],
-        sums[2:6].reshape(2, 2, BLK),
-        moved[2:6].reshape(2, 2, BLK),
-    )
+    def block(shape):
+        if len(shape.shape) == 3 and shape.shape[1] % (CUTS * 16) == 0:
+            return pl.BlockSpec((shape.shape[0], shape.shape[1] // CUTS, shape.shape[2]), lambda c: (0, c, 0))
+        return pl.BlockSpec(shape.shape, lambda c: (0,) * len(shape.shape))
+
+    blocks = [block(shape) for shape in out_shape]
+    return pl.pallas_call(
+        carry_out,
+        name="carry_out",
+        grid=(CUTS,),
+        out_shape=out_shape,
+        in_specs=blocks,
+        out_specs=blocks,
+        compiler_params=pltpu.CompilerParams(vmem_limit_bytes=60 * 2**20),
+    )(*results)
 
 
 def gelu_local(values):
     return jax.nn.gelu(values, approximate=True)
 
 
-def plain(pooled, weight, fc_bias, stitch, cotangent, factor, step_rate):
+def plain(pooled, weight, fc_bias, stitch, cotangent, valid_mask, image_group, step_rate):
     highest = lax.Precision.HIGHEST
-    masked = pooled * factor[None]
+    factor = 1.0 - image_group[None, :].astype(F32) * (1.0 - valid_mask[:, None].astype(F32))
+    masked = pooled * factor.astype(BF16)[None]
     owned = weight.shape[2] // lax.axis_size("wide")
     summed = lax.psum_scatter(
         jnp.einsum("tkc,tkb->ctb", weight, masked, preferred_element_type=F32), "wide", scatter_dimension=0, tiled=True
@@ -751,7 +825,7 @@
     portion = lax.all_gather(pre_low, "wide", axis=0, tiled=True)
     input_sum = jnp.einsum("tkc,ctb->tkb", weight, portion, preferred_element_type=F32)
     block_grad = jnp.einsum("tkb,ctb->tkc", masked, portion, preferred_element_type=F32)
-    pooled_grad = (input_sum * factor.astype(F32)[None]).astype(BF16)
+    pooled_grad = (input_sum * factor[None]).astype(BF16)
     weight_grad = lax.psum_scatter(block_grad, "batch", scatter_dimension=2, tiled=True)
     share = owned // lax.axis_size("batch")
     stitch_mine = lax.dynamic_slice_in_dim(stitch, lax.axis_index("batch") * share, share, 2)
@@ -767,14 +841,14 @@
         and weight.shape[2] == NZ * NX * cotangent.shape[1]
         and pooled.shape[2] % 512 == 0
         and pooled.shape[1] % (16 * PIECES) == 0
+        and pooled.shape[1] % BLK == 0
     )
 
 
 def solution(mesh):
-    def body(pooled, weight, fc_bias, stitch, cotangent, valid_mask, image_group, step_rate):
-        factor = 1.0 - image_group[None, :].astype(F32) * (1.0 - valid_mask[:, None].astype(F32))
+    def body(pooled, weight, fc_bias, stitch, cotangent, *rest):
         form = fused if fits(mesh, pooled, weight, cotangent) else plain
-        return form(pooled, weight, fc_bias, stitch, cotangent, factor.astype(BF16), step_rate)
+        return form(pooled, weight, fc_bias, stitch, cotangent, *rest)
 
     return jax.shard_map(
         body,

time: 423 us -> 367 us (0.87)
  local copies, waits for them, and re-layouts: 50.1 us -> 0 us
  other arithmetic: 15 us -> 0 us
  Pallas kernels: 355 us -> 365 us
    unnamed x7 -> x0, local copies, waits for them, and re-layouts: 30.5 us -> none
    pallas_call x0 -> x1, Pallas kernels: none -> 11.3 us  [fused(): pl.pallas_call(carry_out, name='carry_out', grid=(CUTS,), out_shape=out_s...]
    mul x2 -> x0, other arithmetic: 7.89 us -> none  [the longest x1 5.04 us: fused(): pooled_grad = pooled_raw * factor[None]]
    mul x1 -> x0, local copies, waits for them, and re-layouts: 6.61 us -> none  [fused(): masked = pooled * factor[None]]
    pallas_call x1 -> x0, local copies, waits for them, and re-layouts: 6.61 us -> none  [fused(): pl.pallas_call(functools.partial(kernel, dm), name='stitch_fc6', out_shap...]
    transpose x1 -> x0, other arithmetic: 5.24 us -> none  [fused(): masked_t = jnp.swapaxes(masked, 1, 2)]
where the time goes in v2:
time: 367 us; the launch traced here: 366 us
  Pallas kernels  365 us (99%)
    pallas_call x1, Pallas kernels, fused(): pl.pallas_call(functools.partial(kernel, dm), name='stitch_fc6', out_shap...  354 us
    pallas_call x1, Pallas kernels, fused(): pl.pallas_call(carry_out, name='carry_out', grid=(CUTS,), out_shape=out_s...  11.3 us

profile of v2, /device:TPU:0, one launch (start us, length us, event | category | flops | bytes accessed | tf_op | source)
XLA Modules:
  0.0 366.3 jit_solution(17619525578821719940)
XLA Ops:
  1.3 353.8 %stitch_fc6.1 = (bf16[2,512,1024]{2,1,0:T(8,128)(2,1)}, bf16[2,1152,1024]{2,1,0:T(8,128)(2,1)}, f32[2,1152,1024]{2,1,0:T(8,128)}, f32[2,128]{1,0:T(2,128)}, f32[2,2,128]{2,1,0:T(2,128)}, /*index=5*/f32[2,2,128]{2,1,0:T(2,128)}) custom-call(f32[1]{0:T(128)S(6)} %copy.14.step_ref, bf16[2,1152,4096]{2,1,0:T(8,128)(2,1)} %w_hbm.1, bf16[2,1152,1024]{2,1,0:T(8,128)(2,1)} %p_hbm.1, ...), custom_call_target="tpu_custom_call" | custom-call | flops 57982058496 | bytes 62914560 | tf_op jit(solution)/shard_map/stitch_fc6/pallas_call | solution.py:770
  355.1 11.3 %carry_out.1 = (bf16[2,512,1024]{2,1,0:T(8,128)(2,1)}, bf16[2,1152,1024]{2,1,0:T(8,128)(2,1)}, f32[2,1152,1024]{2,1,0:T(8,128)}, f32[2,128]{1,0:T(2,128)}, f32[2,2,128]{2,1,0:T(2,128)}, /*index=5*/f32[2,2,128]{2,1,0:T(2,128)}) custom-call(bf16[2,512,1024]{2,1,0:T(8,128)(2,1)} %get-tuple-element.12.refs_0_, bf16[2,1152,1024]{2,1,0:T(8,128)(2,1)} %get-tuple-element.13.refs_1_, ...), custom_call_target="tpu_custom_call" | custom-call | tf_op jit(solution)/shard_map/carry_out/pallas_call | solution.py:791

commit v3 on v2

--- a/solution.py
+++ b/solution.py
@@ -27,7 +27,7 @@
         self.subs = self.own // BLK
         self.parts = 2
         self.rows = self.images // self.parts
-        self.rx = (self.rows * 19 // 32) // 16 * 16
+        self.rx = (self.rows * 21 // 32) // 16 * 16
         self.rz = self.rows - self.rx
         self.units = self.towers * self.subs * self.parts
         self.cols = NZ * NX * BLK
@@ -532,7 +532,6 @@
 
         @pl.when(on_a)
         def _():
-            x1_send(a, 0)
             zr_hop(a, 0)
 
         @pl.when((i % 2 == 0) & (i // 2 + 2 < dm.towers * dm.subs))
@@ -543,11 +542,22 @@
         @pl.when(on_b)
         def _():
             z_final(b)
+
+        @pl.when(on_c)
+        def _():
+            gather_arrive(gz_copy, c, 0, False)
+
+        @pl.when(on_p)
+        def _():
+            back_weight(p, 0)
+
+        @pl.when(on_a)
+        def _():
+            x1_send(a, 0)
+
+        @pl.when(on_b)
+        def _():
             x_final(b)
-
-        @pl.when(on_c)
-        def _():
-            gather_arrive(gz_copy, c, 0, False)
 
         @pl.when(on_f)
         def _():
@@ -564,46 +574,58 @@
 
             forward(i + 1, 0)
 
+        @pl.when(on_a)
+        def _():
+            zr_hop(a, 1)
+
+        @pl.when(on_c)
+        def _():
+            gather_arrive(gz_copy, c, 1, False)
+
+        @pl.when(on_f)
+        def _():
+            forward(i + 1, 1)
+
+        @pl.when(on_b)
+        def _():
+            emit(b)
+
+        @pl.when(on_a)
+        def _():
+            x1_send(a, 1)
+            xr_hop(a, 0)
+
+        @pl.when(on_b)
+        def _():
+            gather_arrive(gx_copy, b, 0, True)
+
         @pl.when(on_p)
         def _():
-            back_weight(p, 0)
+            back_weight(p, 1)
 
         @pl.when(on_a)
         def _():
-            x1_send(a, 1)
-            zr_hop(a, 1)
-            xr_hop(a, 0)
+            zr_hop(a, 2)
 
         @pl.when(on_c)
         def _():
-            gather_arrive(gz_copy, c, 1, False)
+            gather_arrive(gz_copy, c, 2, False)
+
+        @pl.when(on_f)
+        def _():
+            forward(i + 1, 2)
+
+        @pl.when(on_a)
+        def _():
+            x1_send(a, 2)
+            xr_hop(a, 1)
 
         @pl.when(on_b)
         def _():
-            gather_arrive(gx_copy, b, 0, True)
-            emit(b)
-
-        @pl.when(on_f)
-        def _():
-            forward(i + 1, 1)
-
-        @pl.when(on_p)
-        def _():
-            back_weight(p, 1)
-
-        @pl.when(on_a)
-        def _():
-            x1_send(a, 2)
-            zr_hop(a, 2)
-            xr_hop(a, 1)
-
-        @pl.when(on_b)
-        def _():
             gather_arrive(gx_copy, b, 1, True)
 
         @pl.when(on_c)
         def _():
-            gather_arrive(gz_copy, c, 2, False)
             gathered(c)
 
         @pl.when(i < n_units // 2)
@@ -615,34 +637,36 @@
                 for j in (0, 1):
                     cot_load(i + 1, j).start()
 
-        @pl.when(on_f)
-        def _():
-            forward(i + 1, 2)
-
         @pl.when(on_p)
         def _():
             back_weight(p, 2)
 
         @pl.when(on_a)
         def _():
-            x1_send(a, 3)
             z_sum(a)
-            xr_hop(a, 2)
 
         @pl.when(on_b)
         def _():
             z4_copy(b).wait_recv()
             for d in (0, 1):
                 gather_hop(gz_copy, b, d, 0)
+
+        @pl.when(on_f)
+        def _():
+            forward(i + 1, 3)
+
+        @pl.when(on_a)
+        def _():
+            x1_send(a, 3)
+            xr_hop(a, 2)
+
+        @pl.when(on_b)
+        def _():
             gather_arrive(gx_copy, b, 2, True)
 
         @pl.when(on_c)
         def _():
             back_pooled(c)
-
-        @pl.when(on_f)
-        def _():
-            forward(i + 1, 3)
 
         for s in (0, 1):
             @pl.when(i == 4 + s)

time: 367 us -> 338 us (0.921)
  Pallas kernels: 365 us -> 336 us
    pallas_call x1, Pallas kernels: 354 us -> 325 us  [fused(): pl.pallas_call(functools.partial(kernel, dm), name='stitch_fc6', out_shap...]
where the time goes in v3:
time: 338 us
  Pallas kernels  336 us (99%)
    pallas_call x1, Pallas kernels, fused(): pl.pallas_call(functools.partial(kernel, dm), name='stitch_fc6', out_shap...  325 us
    pallas_call x1, Pallas kernels, fused(): pl.pallas_call(carry_out, name='carry_out', grid=(CUTS,), out_shape=out_s...  11.3 us

profile of v3, /device:TPU:0, one launch (start us, length us, event | category | flops | bytes accessed | tf_op | source)
XLA Modules:
  0.0 337.8 jit_solution(5560692134654574883)
XLA Ops:
  1.3 325.2 %stitch_fc6.1 = (bf16[2,512,1024]{2,1,0:T(8,128)(2,1)}, bf16[2,1152,1024]{2,1,0:T(8,128)(2,1)}, f32[2,1152,1024]{2,1,0:T(8,128)}, f32[2,128]{1,0:T(2,128)}, f32[2,2,128]{2,1,0:T(2,128)}, /*index=5*/f32[2,2,128]{2,1,0:T(2,128)}) custom-call(f32[1]{0:T(128)S(6)} %copy.14.step_ref, bf16[2,1152,4096]{2,1,0:T(8,128)(2,1)} %w_hbm.1, bf16[2,1152,1024]{2,1,0:T(8,128)(2,1)} %p_hbm.1, ...), custom_call_target="tpu_custom_call" | custom-call | flops 57982058496 | bytes 62914560 | tf_op jit(solution)/shard_map/stitch_fc6/pallas_call | solution.py:794
  326.5 11.3 %carry_out.1 = (bf16[2,512,1024]{2,1,0:T(8,128)(2,1)}, bf16[2,1152,1024]{2,1,0:T(8,128)(2,1)}, f32[2,1152,1024]{2,1,0:T(8,128)}, f32[2,128]{1,0:T(2,128)}, f32[2,2,128]{2,1,0:T(2,128)}, /*index=5*/f32[2,2,128]{2,1,0:T(2,128)}) custom-call(bf16[2,512,1024]{2,1,0:T(8,128)(2,1)} %get-tuple-element.12.refs_0_, bf16[2,1152,1024]{2,1,0:T(8,128)(2,1)} %get-tuple-element.13.refs_1_, ...), custom_call_target="tpu_custom_call" | custom-call | tf_op jit(solution)/shard_map/carry_out/pallas_call | solution.py:815

commit v4 on v2

--- a/solution.py
+++ b/solution.py
@@ -17,6 +17,17 @@
 CUBE = 0.044715
 PIECES = 3
 CUTS = 4
+DRAIN = (
+    "zf0", "xf0", "zf1", "xf1", "hz00", "hz01", "bv0", "gs0", "gx00", "gs1", "gx01", "hz10", "hz11", "bv1", "em",
+    "gz00", "gx10", "gz01", "gx11", "hz20", "hz21", "hd", "bv2", "gz10", "gx20", "gz11", "gx21", "hp0", "hp1", "hp2",
+    "ss", "bw0", "bw1", "bw2", "gz20", "gz21", "gd", "bp0", "bp1", "bp2", "bx0", "bx1", "bx2",
+)
+ORDER = (
+    "zr00", "ws", "zf0", "gz00", "bw0", "x10", "xf0", "ww", "p0", "zr01", "zf1", "gz01", "xf1", "f0",
+    "zr10", "gz10", "f1", "x11", "xr00", "gx00", "zr11", "gz11", "bw1", "xr01", "gx01", "em",
+    "zr20", "gz20", "f2", "x12", "xr10", "gx10", "ct", "zr21", "gz21", "bw2", "xr11", "gx11", "gd",
+    "zs0", "gs0", "f3", "x13", "xr20", "gx20", "bp0", "zs1", "gs1", "bp1", "xr21", "gx21", "bp2",
+)
 
 
 class Dims:
@@ -44,12 +55,15 @@
     s_hbm, pg_hbm, wg_hbm, out_b, out_sg, out_sn,
     wb, xt, xb, xpb, hole, small_img, craw, cot, stmp, sbuf, acc, fwd, gat, gatp,
     x1_s, x1_r, xr_s, xr_r, zr_s, zr_r, zown, z2_s, z2_r,
-    own, y_s, y_r, hid0, htmp, pgb, sacc, sum_s, sum_r,
+    own, tacc, y_s, y_r, hid0, htmp, pgb, sacc, sum_s, sum_r,
     m_w, m_ld, m_x1s, m_x1r, m_xrs, m_xrr, m_zrs, m_zrr, m_z2s, m_z2r, m_z4s, m_z4r,
     m_gxs, m_gxr, m_gzs, m_gzr, m_x5s, m_x5r, m_cs, m_cr, m_ys, m_yr, m_ss, m_sr, m_xps, m_xpr, m_own, m_pg,
     m_cot, m_out,
 ):
     n_units, rows, rx, rz = dm.units, dm.rows, dm.rx, dm.rz
+    mid_x, mid_z = rx // 32 * 16, rz // 32 * 16
+    cuts_x = (0, mid_x), (mid_x, rx - mid_x)
+    cuts_z = (0, mid_z), (mid_z, rz - mid_z)
     wi, bi = lax.axis_index("wide"), lax.axis_index("batch")
     z, x = wi // NX, wi % NX
     y, core = bi // 2, bi % 2
@@ -67,7 +81,7 @@
         return pltpu.make_async_remote_copy(src, dst, ss, rs, device_id=dev, device_id_type=MESH)
 
     def al(v, k=BLK):
-        return pl.multiple_of(v, k)
+        return v if isinstance(v, int) else pl.multiple_of(v, k)
 
     def tower(n):
         return n // (dm.subs * dm.parts)
@@ -110,35 +124,41 @@
     def x1_copy(n, o):
         return rc(x1_s.at[o], x1_r.at[n % 2, o], m_x1s.at[o], m_x1r.at[n % 2, o], x_dev)
 
-    def xr_copy(n, d, h):
-        return rc(xr_s.at[d, h], xr_r.at[n % 2, d, h], m_xrs.at[d, h], m_xrr.at[n % 2, d, h], z_dev(d))
-
-    def zr_copy(n, d, h):
-        return rc(zr_s.at[d, h], zr_r.at[n % 2, d, h], m_zrs.at[d, h], m_zrr.at[n % 2, d, h], z_dev(d))
-
-    def z2_copy(n):
-        return rc(z2_s, z2_r.at[n % 2], m_z2s, m_z2r.at[n % 2], x_dev)
-
-    def g_x(n, o, xx):
-        return gat.at[gpair(n), pl.ds(al(part(n) * rows, 16), rx), pl.ds(col(o, xx), BLK)]
-
-    def g_z(n, o, xx, width):
-        return gat.at[gpair(n), pl.ds(al(part(n) * rows + rx, 16), rz), pl.ds(col(o, xx), width)]
-
-    def z4_copy(n):
-        return rc(g_z(n, z, x, BLK), g_z(n, z, x, BLK), m_z4s, m_z4r.at[n % 2], x_dev)
-
-    def gx_copy(n, d, h):
-        o = z - h if d == 0 else z + h
-        return rc(g_x(n, o, x), g_x(n, o, x), m_gxs.at[d, h], m_gxr.at[n % 2, d, h], z_dev(d))
-
-    def gz_copy(n, d, h):
-        o = z - h if d == 0 else z + h
-        blk = g_z(n, o, 0, NX * BLK)
-        return rc(blk, blk, m_gzs.at[d, h], m_gzr.at[n % 2, d, h], z_dev(d))
-
-    def x5_copy(n, o, xx):
-        return rc(g_x(n, o, xx), g_x(n, o, xx), m_x5s.at[o], m_x5r.at[n % 2, o], x_dev)
+    def xr_copy(n, d, h, f):
+        cut = pl.ds(*cuts_x[f])
+        return rc(xr_s.at[d, h, cut], xr_r.at[n % 2, d, h, cut], m_xrs.at[d, h, f], m_xrr.at[n % 2, d, h, f], z_dev(d))
+
+    def zr_copy(n, d, h, f):
+        cut = pl.ds(*cuts_z[f])
+        return rc(zr_s.at[d, h, cut], zr_r.at[n % 2, d, h, cut], m_zrs.at[d, h, f], m_zrr.at[n % 2, d, h, f], z_dev(d))
+
+    def z2_copy(n, f):
+        cut = pl.ds(*cuts_z[f])
+        return rc(z2_s.at[cut], z2_r.at[n % 2, cut], m_z2s.at[f], m_z2r.at[n % 2, f], x_dev)
+
+    def g_x(n, o, xx, f):
+        start, size = cuts_x[f]
+        return gat.at[gpair(n), pl.ds(al(part(n) * rows + start, 16), size), pl.ds(col(o, xx), BLK)]
+
+    def g_z(n, o, xx, width, f):
+        start, size = cuts_z[f]
+        return gat.at[gpair(n), pl.ds(al(part(n) * rows + rx + start, 16), size), pl.ds(col(o, xx), width)]
+
+    def z4_copy(n, f):
+        blk = g_z(n, z, x, BLK, f)
+        return rc(blk, blk, m_z4s.at[f], m_z4r.at[n % 2, f], x_dev)
+
+    def gx_copy(n, d, h, f):
+        blk = g_x(n, z - h if d == 0 else z + h, x, f)
+        return rc(blk, blk, m_gxs.at[d, h, f], m_gxr.at[n % 2, d, h, f], z_dev(d))
+
+    def gz_copy(n, d, h, f):
+        blk = g_z(n, z - h if d == 0 else z + h, 0, NX * BLK, f)
+        return rc(blk, blk, m_gzs.at[d, h, f], m_gzr.at[n % 2, d, h, f], z_dev(d))
+
+    def x5_copy(n, o, xx, f):
+        blk = g_x(n, o, xx, f)
+        return rc(blk, blk, m_x5s.at[o, f], m_x5r.at[n % 2, o, f], x_dev)
 
     def c_copy(n, e):
         r = pl.ds(al(part(n) * rows, 16), rows)
@@ -208,30 +228,34 @@
             x1_s[o, r : r + m] = fwd[n % 2, r : r + m, pl.ds(col(o, 1 - x), BLK)].astype(BF16)
         x1_copy(n, o).start()
 
-    def xr_hop(n, h):
+    def xr_hop(n, h, f):
+        start, size = cuts_x[f]
         for d in (0, 1):
             o = 3 - h + z if d == 0 else h - 3 + z
 
             @pl.when(far(d) <= h)
             def _():
-                x1_copy(n, o).wait_recv()
+                if f == 0:
+                    x1_copy(n, o).wait_recv()
                 if h:
                     @pl.when(far(d) >= 1)
                     def _():
-                        xr_copy(n, d, h - 1).wait_recv()
+                        xr_copy(n, d, h - 1, f).wait_recv()
 
                 @pl.when(n >= 1)
                 def _():
-                    xr_copy(n, d, h).wait_send()
-
-                for r, m in chunks(rx):
+                    xr_copy(n, d, h, f).wait_send()
+
+                for r, m in chunks(size):
+                    r += start
                     v = fwd[n % 2, r : r + m, pl.ds(col(o, x), BLK)] + x1_r[n % 2, o, r : r + m].astype(F32)
                     if h:
                         v = v + xr_r[n % 2, d, h - 1, r : r + m].astype(F32)
                     xr_s[d, h, r : r + m] = v.astype(BF16)
-                xr_copy(n, d, h).start()
-
-    def zr_hop(n, h):
+                xr_copy(n, d, h, f).start()
+
+    def zr_hop(n, h, f):
+        start, size = cuts_z[f]
         for d in (0, 1):
             o = 3 - h + z if d == 0 else h - 3 + z
 
@@ -240,31 +264,34 @@
                 if h:
                     @pl.when(far(d) >= 1)
                     def _():
-                        zr_copy(n, d, h - 1).wait_recv()
+                        zr_copy(n, d, h - 1, f).wait_recv()
 
                 @pl.when(n >= 1)
                 def _():
-                    zr_copy(n, d, h).wait_send()
-
-                for r, m in chunks(rz):
+                    zr_copy(n, d, h, f).wait_send()
+
+                for r, m in chunks(size):
+                    r += start
                     v = fwd[n % 2, rx + r : rx + r + m, pl.ds(col(o, 0), NX * BLK)]
                     if h:
                         v = v + zr_r[n % 2, d, h - 1, r : r + m].astype(F32)
                     zr_s[d, h, r : r + m] = v.astype(BF16)
-                zr_copy(n, d, h).start()
-
-    def z_sum(n):
+                zr_copy(n, d, h, f).start()
+
+    def z_sum(n, f):
         for d in (0, 1):
             @pl.when(far(d) >= 1)
             def _():
-                zr_copy(n, d, 2).wait_recv()
+                zr_copy(n, d, 2, f).wait_recv()
 
         @pl.when(n >= 1)
         def _():
-            z2_copy(n).wait_send()
-
+            z2_copy(n, f).wait_send()
+
+        start, size = cuts_z[f]
         for xx in (1 - x, x):
-            for r, m in chunks(rz):
+            for r, m in chunks(size):
+                r += start
                 lanes = pl.ds(al(xx * BLK), BLK)
                 v = (
                     fwd[n % 2, rx + r : rx + r + m, pl.ds(col(z, xx), BLK)]
@@ -276,7 +303,7 @@
                 else:
                     z2_s[r : r + m] = v.astype(BF16)
             if xx is not x:
-                z2_copy(n).start()
+                z2_copy(n, f).start()
 
     def finish(n, row0, count, total):
         t, u = tower(n), sub(n)
@@ -330,25 +357,35 @@
                 sbuf[n % 2, i] = stmp[i].T
                 s_copy(n, i).start()
 
-    def z_final(n):
-        z2_copy(n).wait_recv()
-        finish(n, rx, rz, lambda r, m: zown[r : r + m] + z2_r[n % 2, r : r + m].astype(F32))
+    def z_final(n, f):
+        z2_copy(n, f).wait_recv()
+        start, size = cuts_z[f]
+
+        def total(r, m):
+            r += start
+            return zown[r : r + m] + z2_r[n % 2, r : r + m].astype(F32)
+
+        finish(n, rx + start, size, total)
 
         @pl.when(n >= 1)
         def _():
-            z4_copy(n).wait_send()
-
-        z4_copy(n).start()
-        mix(n, rx, rz)
-
-    def x_final(n):
-        x1_copy(n, z).wait_recv()
+            z4_copy(n, f).wait_send()
+
+        z4_copy(n, f).start()
+        mix(n, rx + start, size)
+
+    def x_final(n, f):
+        if f == 0:
+            x1_copy(n, z).wait_recv()
         for d in (0, 1):
             @pl.when(far(d) >= 1)
             def _():
-                xr_copy(n, d, 2).wait_recv()
+                xr_copy(n, d, 2, f).wait_recv()
+
+        start, size = cuts_x[f]
 
         def total(r, m):
+            r += start
             return (
                 fwd[n % 2, r : r + m, pl.ds(col(z, x), BLK)]
                 + x1_r[n % 2, z, r : r + m].astype(F32)
@@ -356,41 +393,47 @@
                 + xr_r[n % 2, 1, 2, r : r + m].astype(F32)
             )
 
-        finish(n, 0, rx, total)
+        finish(n, start, size, total)
         for d in (0, 1):
-            gather_hop(gx_copy, n, d, 0)
-        x5_send(n, z)
-        mix(n, 0, rx)
-
-    def gather_hop(copy, n, d, h):
+            gather_hop(gx_copy, n, d, 0, f)
+        x5_send(n, z, f)
+        mix(n, start, size)
+
+    def gather_hop(copy, n, d, h, f):
         @pl.when((far(d) >= h) & (far(d) <= 2))
         def _():
             @pl.when(n >= 1)
             def _():
-                copy(n, d, h).wait_send()
-
-            copy(n, d, h).start()
-
-    def x5_send(n, o):
+                copy(n, d, h, f).wait_send()
+
+            copy(n, d, h, f).start()
+
+    def x5_send(n, o, f):
         @pl.when(n >= 1)
         def _():
-            x5_copy(n, o, x).wait_send()
-
-        x5_copy(n, o, x).start()
-
-    def gather_arrive(copy, n, h, forward_x):
+            x5_copy(n, o, x, f).wait_send()
+
+        x5_copy(n, o, x, f).start()
+
+    def gz_first(n, f):
+        z4_copy(n, f).wait_recv()
+        for d in (0, 1):
+            gather_hop(gz_copy, n, d, 0, f)
+
+    def gather_arrive(copy, n, h, forward_x, f):
         for d in (0, 1):
             @pl.when(far(d) >= h + 1)
             def _():
-                copy(n, d, h).wait_recv()
+                copy(n, d, h, f).wait_recv()
                 if h < 2:
-                    gather_hop(copy, n, d, h + 1)
+                    gather_hop(copy, n, d, h + 1, f)
                 if forward_x:
-                    x5_send(n, z - 1 - h if d == 0 else z + 1 + h)
+                    x5_send(n, z - 1 - h if d == 0 else z + 1 + h, f)
 
     def gathered(n):
         for o in range(NZ):
-            x5_copy(n, o, 1 - x).wait_recv()
+            for f in (0, 1):
+                x5_copy(n, o, 1 - x, f).wait_recv()
         for e in (0, 1):
             @pl.when(n >= 1)
             def _():
@@ -398,19 +441,18 @@
 
             c_copy(n, e).start()
 
-    def back_pooled(n):
+    def back_pooled(n, q):
         t, s = tower(n), part(n)
         lanes = pl.ds(al(s * rows), rows)
-
-        @pl.loop(0, PIECES)
-        def _(q):
-            k = pl.ds(al(q * dm.third, 16), dm.third)
-            acc[k, lanes] += lax.dot_general(
-                wb[(n // dm.parts) % 4, k, :],
-                gat[gpair(n), pl.ds(al(s * rows, 16), rows), :],
-                NT,
-                preferred_element_type=F32,
-            )
+        k = pl.ds(q * dm.third, dm.third)
+        acc[k, lanes] += lax.dot_general(
+            wb[(n // dm.parts) % 4, k, :],
+            gat[gpair(n), pl.ds(al(s * rows, 16), rows), :],
+            NT,
+            preferred_element_type=F32,
+        )
+        if q < PIECES - 1:
+            return
 
         @pl.when(sub(n) == dm.subs - 1)
         def _():
@@ -435,37 +477,46 @@
         for e in (0, 1):
             own_copy(p, q, e).start()
 
-    def back_weight(p, q):
+    def back_weight(n, q):
+        t, s, p = tower(n), part(n), n // dm.parts
+        k, imgs = pl.ds(q * dm.third, dm.third), pl.ds(al(part(n) * rows), rows)
         if q == 0:
-            for n in (2 * p, 2 * p + 1):
-                for e in (0, 1):
-                    c_copy(n, e).wait_recv()
-
-            @pl.when(p % dm.subs == 0)
-            def _():
-                xp_copy(p // dm.subs).wait_recv()
-
-        @pl.when(p >= 1)
-        def _():
-            y_arrive(p - 1, q)
-            y_copy(p, q).wait_send()
-
-        @pl.when(p >= 2)
-        def _():
             for e in (0, 1):
-                own_copy(p, q, e).wait()
-
-        t, k = p // dm.subs, pl.ds(q * dm.third, dm.third)
+                c_copy(n, e).wait_recv()
+
+            @pl.when((s == 0) & (p % dm.subs == 0))
+            def _():
+                xp_copy(t).wait_recv()
 
         def grads(yy):
             lanes = pl.ds(col(2 * yy + core, 0), NX * BLK)
-            return jnp.dot(xb[t, k, :], gat[p % 2, :, lanes], preferred_element_type=F32) + jnp.dot(
-                xpb[t, k, :], gatp[p % 2, :, pl.ds(al(yy * NX * BLK), NX * BLK)], preferred_element_type=F32
+            return jnp.dot(xb[t, k, imgs], gat[p % 2, imgs, lanes], preferred_element_type=F32) + jnp.dot(
+                xpb[t, k, imgs], gatp[p % 2, imgs, pl.ds(al(yy * NX * BLK), NX * BLK)], preferred_element_type=F32
             )
 
-        y_s[k, :] = grads(1 - y).astype(BF16)
-        y_copy(p, q).start()
-        own[p % 2, k, :] = grads(y)
+        @pl.when(s == 0)
+        def _():
+            @pl.when(p >= 1)
+            def _():
+                y_arrive(p - 1, q)
+
+            @pl.when(p >= 2)
+            def _():
+                for e in (0, 1):
+                    own_copy(p, q, e).wait()
+
+            tacc[k, :] = grads(1 - y)
+            own[p % 2, k, :] = grads(y)
+
+        @pl.when(s == 1)
+        def _():
+            @pl.when(p >= 1)
+            def _():
+                y_copy(p - 1, q).wait_send()
+
+            y_s[k, :] = (tacc[k, :] + grads(1 - y)).astype(BF16)
+            y_copy(p, q).start()
+            own[p % 2, k, :] += grads(y)
 
     def sums_send():
         for u in range(dm.subs):
@@ -523,91 +574,24 @@
 
     def tick(i, carry):
         a, b, c = i, i - 1, i - 2
-        on_a = i < n_units
-        on_b = (i >= 1) & (i <= n_units)
-        on_c = (i >= 2) & (i <= n_units + 1)
+        on_a, on_b, on_c = i >= 0, i >= 1, i >= 2
         on_f = i + 1 < n_units
-        p = lax.div(i - 4, 2)
-        on_p = (i >= 4) & (i % 2 == 0)
-
-        @pl.when(on_a)
-        def _():
-            x1_send(a, 0)
-            zr_hop(a, 0)
-
-        @pl.when((i % 2 == 0) & (i // 2 + 2 < dm.towers * dm.subs))
-        def _():
+        on_p = i >= 3
+
+        def w_start():
             for w in range(NZ * NX):
                 w_load(i // 2 + 2, w).start()
 
-        @pl.when(on_b)
-        def _():
-            z_final(b)
-            x_final(b)
-
-        @pl.when(on_c)
-        def _():
-            gather_arrive(gz_copy, c, 0, False)
-
-        @pl.when(on_f)
-        def _():
-            @pl.when(i % 2 == 1)
-            def _():
-                for w in range(NZ * NX):
-                    w_load((i + 1) // 2, w).wait()
-
-            @pl.when(i == 0)
-            def _():
-                x_load(0, 1).wait()
-                prepare(0, 1)
-                xp_copy(0).start()
-
-            forward(i + 1, 0)
-
-        @pl.when(on_p)
-        def _():
-            back_weight(p, 0)
-
-        @pl.when(on_a)
-        def _():
-            x1_send(a, 1)
-            zr_hop(a, 1)
-            xr_hop(a, 0)
-
-        @pl.when(on_c)
-        def _():
-            gather_arrive(gz_copy, c, 1, False)
-
-        @pl.when(on_b)
-        def _():
-            gather_arrive(gx_copy, b, 0, True)
-            emit(b)
-
-        @pl.when(on_f)
-        def _():
-            forward(i + 1, 1)
-
-        @pl.when(on_p)
-        def _():
-            back_weight(p, 1)
-
-        @pl.when(on_a)
-        def _():
-            x1_send(a, 2)
-            zr_hop(a, 2)
-            xr_hop(a, 1)
-
-        @pl.when(on_b)
-        def _():
-            gather_arrive(gx_copy, b, 1, True)
-
-        @pl.when(on_c)
-        def _():
-            gather_arrive(gz_copy, c, 2, False)
-            gathered(c)
-
-        @pl.when(i < n_units // 2)
-        def _():
+        def w_wait():
+            for w in range(NZ * NX):
+                w_load((i + 1) // 2, w).wait()
+
+        def first_images():
+            x_load(0, 1).wait()
+            prepare(0, 1)
+            xp_copy(0).start()
+
+        def cot_next():
             prepare_cot(i)
 
             @pl.when(i + 1 < n_units // 2)
@@ -615,34 +599,32 @@
                 for j in (0, 1):
                     cot_load(i + 1, j).start()
 
-        @pl.when(on_f)
-        def _():
-            forward(i + 1, 2)
-
-        @pl.when(on_p)
-        def _():
-            back_weight(p, 2)
-
-        @pl.when(on_a)
-        def _():
-            x1_send(a, 3)
-            z_sum(a)
-            xr_hop(a, 2)
-
-        @pl.when(on_b)
-        def _():
-            z4_copy(b).wait_recv()
-            for d in (0, 1):
-                gather_hop(gz_copy, b, d, 0)
-            gather_arrive(gx_copy, b, 2, True)
-
-        @pl.when(on_c)
-        def _():
-            back_pooled(c)
-
-        @pl.when(on_f)
-        def _():
-            forward(i + 1, 3)
+        steps = {
+            "ws": ((i % 2 == 0) & (i // 2 + 2 < dm.towers * dm.subs), w_start),
+            "ww": (on_f & (i % 2 == 1), w_wait),
+            "p0": (i == 0, first_images),
+            "ct": (i < n_units // 2, cot_next),
+            "em": (on_b, lambda: emit(b)),
+            "gd": (on_c, lambda: gathered(c)),
+        }
+        for q in range(4):
+            steps[f"x1{q}"] = on_a, functools.partial(x1_send, a, q)
+            steps[f"f{q}"] = on_f, functools.partial(forward, i + 1, q)
+        for h in range(PIECES):
+            steps[f"bw{h}"] = on_p, functools.partial(back_weight, i - 3, h)
+            steps[f"bp{h}"] = on_c, functools.partial(back_pooled, c, h)
+        for f in (0, 1):
+            steps[f"zf{f}"] = on_b, functools.partial(z_final, b, f)
+            steps[f"xf{f}"] = on_b, functools.partial(x_final, b, f)
+            steps[f"zs{f}"] = on_a, functools.partial(z_sum, a, f)
+            steps[f"gs{f}"] = on_b, functools.partial(gz_first, b, f)
+            for h in range(3):
+                steps[f"zr{h}{f}"] = on_a, functools.partial(zr_hop, a, h, f)
+                steps[f"xr{h}{f}"] = on_a, functools.partial(xr_hop, a, h, f)
+                steps[f"gx{h}{f}"] = on_b, functools.partial(gather_arrive, gx_copy, b, h, True, f)
+                steps[f"gz{h}{f}"] = on_c, functools.partial(gather_arrive, gz_copy, c, h, False, f)
+        for name in ORDER:
+            pl.when(steps[name][0])(steps[name][1])
 
         for s in (0, 1):
             @pl.when(i == 4 + s)
@@ -652,15 +634,34 @@
                 if s:
                     xp_copy(1).start()
 
-        @pl.when(i == n_units)
-        def _():
-            sums_send()
-
         return carry
 
-    lax.fori_loop(0, n_units + 3, tick, 0)
+    lax.fori_loop(0, n_units, tick, 0)
 
     last, pairs = n_units - 1, dm.towers * dm.subs
+    ends = {
+        "em": lambda: emit(last),
+        "hd": lambda: gathered(last - 1),
+        "gd": lambda: gathered(last),
+        "ss": sums_send,
+    }
+    for q in range(PIECES):
+        ends[f"bv{q}"] = functools.partial(back_weight, last - 2, q)
+        ends[f"bw{q}"] = functools.partial(back_weight, last - 1, q)
+        ends[f"bx{q}"] = functools.partial(back_weight, last, q)
+        ends[f"hp{q}"] = functools.partial(back_pooled, last - 1, q)
+        ends[f"bp{q}"] = functools.partial(back_pooled, last, q)
+    for f in (0, 1):
+        ends[f"zf{f}"] = functools.partial(z_final, last, f)
+        ends[f"xf{f}"] = functools.partial(x_final, last, f)
+        ends[f"gs{f}"] = functools.partial(gz_first, last, f)
+        for h in range(3):
+            ends[f"gx{h}{f}"] = functools.partial(gather_arrive, gx_copy, last, h, True, f)
+            ends[f"gz{h}{f}"] = functools.partial(gather_arrive, gz_copy, last, h, False, f)
+            ends[f"hz{h}{f}"] = functools.partial(gather_arrive, gz_copy, last - 1, h, False, f)
+    for name in DRAIN:
+        ends[name]()
+
     for k in (1, 2, 3):
         sum_copy(k).wait_recv()
     total = sum_s[bi] + sum_r[0] + sum_r[1] + sum_r[2]
@@ -687,20 +688,22 @@
         c_copy(last, e).wait_send()
     for o in range(NZ):
         x1_copy(last, o).wait_send()
-        x5_copy(last, o, x).wait_send()
-    z2_copy(last).wait_send()
-    z4_copy(last).wait_send()
-    for d in (0, 1):
-        for h in range(3):
-            @pl.when(far(d) <= h)
-            def _():
-                xr_copy(last, d, h).wait_send()
-                zr_copy(last, d, h).wait_send()
-
-            @pl.when((far(d) >= h) & (far(d) <= 2))
-            def _():
-                gx_copy(last, d, h).wait_send()
-                gz_copy(last, d, h).wait_send()
+    for f in (0, 1):
+        for o in range(NZ):
+            x5_copy(last, o, x, f).wait_send()
+        z2_copy(last, f).wait_send()
+        z4_copy(last, f).wait_send()
+        for d in (0, 1):
+            for h in range(3):
+                @pl.when(far(d) <= h)
+                def _():
+                    xr_copy(last, d, h, f).wait_send()
+                    zr_copy(last, d, h, f).wait_send()
+
+                @pl.when((far(d) >= h) & (far(d) <= 2))
+                def _():
+                    gx_copy(last, d, h, f).wait_send()
+                    gz_copy(last, d, h, f).wait_send()
 
 
 def carry_out(*refs):
@@ -740,6 +743,7 @@
         vm((rz, BLK), BF16),
         vm((2, rz, BLK), BF16),
         vm((2, feats, NX * BLK), F32),
+        vm((feats, NX * BLK), F32),
         vm((feats, NX * BLK), BF16),
         vm((2, feats, NX * BLK), BF16),
         vm((images, own), F32),
@@ -751,9 +755,9 @@
     ] + [
         dma(shape)
         for shape in (
-            (4, NZ * NX), (2, 2), (NZ,), (2, NZ), (2, 3), (2, 2, 3), (2, 3), (2, 2, 3), (), (2,), (), (2,),
-            (2, 3), (2, 2, 3), (2, 3), (2, 2, 3), (NZ,), (2, NZ), (2,), (4, 2), (PIECES,), (2, PIECES), (3,), (3,), (2,), (2,),
-            (2, PIECES, 2), (), (2, 2), (2, 2),
+            (4, NZ * NX), (2, 2), (NZ,), (2, NZ), (2, 3, 2), (2, 2, 3, 2), (2, 3, 2), (2, 2, 3, 2), (2,), (2, 2), (2,), (2, 2),
+            (2, 3, 2), (2, 2, 3, 2), (2, 3, 2), (2, 2, 3, 2), (NZ, 2), (2, NZ, 2), (2,), (4, 2), (PIECES,), (2, PIECES), (3,), (3,),
+            (2,), (2,), (2, PIECES, 2), (), (2, 2), (2, 2),
         )
     ]
     anyspace = pl.BlockSpec(memory_space=pl.ANY)

time: 367 us -> 319 us (0.87)
  Pallas kernels: 365 us -> 317 us
    pallas_call x1, Pallas kernels: 354 us -> 306 us  [fused(): pl.pallas_call(functools.partial(kernel, dm), name='stitch_fc6', out_shap...]
where the time goes in v4:
time: 319 us
  Pallas kernels  317 us (99%)
    pallas_call x1, Pallas kernels, fused(): pl.pallas_call(functools.partial(kernel, dm), name='stitch_fc6', out_shap...  306 us
    pallas_call x1, Pallas kernels, fused(): pl.pallas_call(carry_out, name='carry_out', grid=(CUTS,), out_shape=out_s...  11.3 us

profile of v4, /device:TPU:0, one launch (start us, length us, event | category | flops | bytes accessed | tf_op | source)
XLA Modules:
  0.0 318.8 jit_solution(6421717241893622028)
XLA Ops:
  1.3 306.2 %stitch_fc6.1 = (bf16[2,512,1024]{2,1,0:T(8,128)(2,1)}, bf16[2,1152,1024]{2,1,0:T(8,128)(2,1)}, f32[2,1152,1024]{2,1,0:T(8,128)}, f32[2,128]{1,0:T(2,128)}, f32[2,2,128]{2,1,0:T(2,128)}, /*index=5*/f32[2,2,128]{2,1,0:T(2,128)}) custom-call(f32[1]{0:T(128)S(6)} %copy.14.step_ref, bf16[2,1152,4096]{2,1,0:T(8,128)(2,1)} %w_hbm.1, bf16[2,1152,1024]{2,1,0:T(8,128)(2,1)} %p_hbm.1, ...), custom_call_target="tpu_custom_call" | custom-call | flops 57982058496 | bytes 62914560 | tf_op jit(solution)/shard_map/stitch_fc6/pallas_call | solution.py:774
  307.4 11.3 %carry_out.1 = (bf16[2,512,1024]{2,1,0:T(8,128)(2,1)}, bf16[2,1152,1024]{2,1,0:T(8,128)(2,1)}, f32[2,1152,1024]{2,1,0:T(8,128)}, f32[2,128]{1,0:T(2,128)}, f32[2,2,128]{2,1,0:T(2,128)}, /*index=5*/f32[2,2,128]{2,1,0:T(2,128)}) custom-call(bf16[2,512,1024]{2,1,0:T(8,128)(2,1)} %get-tuple-element.12.refs_0_, bf16[2,1152,1024]{2,1,0:T(8,128)(2,1)} %get-tuple-element.13.refs_1_, ...), custom_call_target="tpu_custom_call" | custom-call | tf_op jit(solution)/shard_map/carry_out/pallas_call | solution.py:795

commit v5 on v4

--- a/solution.py
+++ b/solution.py
@@ -23,10 +23,10 @@
     "ss", "bw0", "bw1", "bw2", "gz20", "gz21", "gd", "bp0", "bp1", "bp2", "bx0", "bx1", "bx2",
 )
 ORDER = (
-    "zr00", "ws", "zf0", "gz00", "bw0", "x10", "xf0", "ww", "p0", "zr01", "zf1", "gz01", "xf1", "f0",
-    "zr10", "gz10", "f1", "x11", "xr00", "gx00", "zr11", "gz11", "bw1", "xr01", "gx01", "em",
-    "zr20", "gz20", "f2", "x12", "xr10", "gx10", "ct", "zr21", "gz21", "bw2", "xr11", "gx11", "gd",
-    "zs0", "gs0", "f3", "x13", "xr20", "gx20", "bp0", "zs1", "gs1", "bp1", "xr21", "gx21", "bp2",
+    "zr00", "ws", "zf0", "gz00", "bw0", "x10", "xf0", "ww", "p0", "zr01", "zf1", "gz01", "bw1", "xf1", "f0",
+    "zr10", "gz10", "f1", "x11", "xr00", "gx00", "em", "zr11", "gz11", "bw2", "xr01", "gx01", "f2",
+    "zr20", "gz20", "ct", "az", "x12", "xr10", "gx10", "f3", "zr21", "gz21", "gd", "bp0", "xr11", "gx11",
+    "zs0", "gs0", "x13", "xr20", "gx20", "bp1", "zs1", "gs1", "bp2", "xr21", "gx21",
 )
 
 
@@ -52,13 +52,13 @@
 def kernel(
     dm,
     step_ref, w_hbm, p_hbm, c_hbm, bias, st, valid, group,
-    s_hbm, pg_hbm, wg_hbm, out_b, out_sg, out_sn,
+    s_hbm, pg_hbm, wg_hbm, out_b, out_sg, out_sn, mine_hbm, theirs_hbm,
     wb, xt, xb, xpb, hole, small_img, craw, cot, stmp, sbuf, acc, fwd, gat, gatp,
     x1_s, x1_r, xr_s, xr_r, zr_s, zr_r, zown, z2_s, z2_r,
     own, tacc, y_s, y_r, hid0, htmp, pgb, sacc, sum_s, sum_r,
     m_w, m_ld, m_x1s, m_x1r, m_xrs, m_xrr, m_zrs, m_zrr, m_z2s, m_z2r, m_z4s, m_z4r,
     m_gxs, m_gxr, m_gzs, m_gzr, m_x5s, m_x5r, m_cs, m_cr, m_ys, m_yr, m_ss, m_sr, m_xps, m_xpr, m_own, m_pg,
-    m_cot, m_out,
+    m_cot, m_out, m_last,
 ):
     n_units, rows, rx, rz = dm.units, dm.rows, dm.rx, dm.rz
     mid_x, mid_z = rx // 32 * 16, rz // 32 * 16
@@ -179,6 +179,13 @@
             own.at[p % 2, k, pl.ds(e * BLK, BLK)],
             wg_hbm.at[t, k, pl.ds(al(e * dm.own + u * BLK), BLK)],
             m_own.at[p % 2, q, e],
+        )
+
+    def last_copies(q):
+        k = pl.ds(q * dm.third, dm.third)
+        return (
+            pltpu.make_async_copy(y_s.at[k], theirs_hbm.at[k], m_last.at[q, 0]),
+            pltpu.make_async_copy(own.at[(dm.towers * dm.subs - 1) % 2, k], mine_hbm.at[k], m_last.at[q, 1]),
         )
 
     def pg_copy(t, s):
@@ -479,6 +486,7 @@
 
     def back_weight(n, q):
         t, s, p = tower(n), part(n), n // dm.parts
+        is_last = isinstance(n, int) and n == n_units - 1
         k, imgs = pl.ds(q * dm.third, dm.third), pl.ds(al(part(n) * rows), rows)
         if q == 0:
             for e in (0, 1):
@@ -515,8 +523,12 @@
                 y_copy(p - 1, q).wait_send()
 
             y_s[k, :] = (tacc[k, :] + grads(1 - y)).astype(BF16)
-            y_copy(p, q).start()
+            if not is_last:
+                y_copy(p, q).start()
             own[p % 2, k, :] += grads(y)
+            if is_last:
+                for copy in last_copies(q):
+                    copy.start()
 
     def sums_send():
         for u in range(dm.subs):
@@ -553,10 +565,6 @@
     x_load(0, 0).wait()
     prepare(0, 0)
 
-    @pl.loop(0, dm.feats // 8)
-    def _(k):
-        acc[pl.ds(al(k * 8, 8), 8)] = jnp.zeros((8, dm.images), F32)
-
     for d in (0, 1):
         @pl.when(far(d) == 0)
         def _():
@@ -578,6 +586,11 @@
         on_f = i + 1 < n_units
         on_p = i >= 3
 
+        def clear():
+            @pl.loop(0, dm.feats // 32)
+            def _(k):
+                acc[pl.ds(al(k * 32, 32), 32)] = jnp.zeros((32, dm.images), F32)
+
         def w_start():
             for w in range(NZ * NX):
                 w_load(i // 2 + 2, w).start()
@@ -602,6 +615,7 @@
         steps = {
             "ws": ((i % 2 == 0) & (i // 2 + 2 < dm.towers * dm.subs), w_start),
             "ww": (on_f & (i % 2 == 1), w_wait),
+            "az": (i == 0, clear),
             "p0": (i == 0, first_images),
             "ct": (i < n_units // 2, cot_next),
             "em": (on_b, lambda: emit(b)),
@@ -670,12 +684,10 @@
         out_sg[i] = total[2 + 2 * i : 4 + 2 * i]
         out_sn[i] = st[i, :, pl.ds(al(bi * BLK), BLK)] - step_ref[0] * total[2 + 2 * i : 4 + 2 * i]
     for q in range(PIECES):
-        y_arrive(pairs - 1, q)
-    for q in range(PIECES):
         for e in (0, 1):
             own_copy(pairs - 2, q, e).wait()
-            own_copy(pairs - 1, q, e).wait()
-        y_copy(pairs - 1, q).wait_send()
+        for copy in last_copies(q):
+            copy.wait()
     pg_copy(1, 1).wait()
     for i in (0, 1):
         s_copy(last - 1, i).wait()
@@ -710,6 +722,42 @@
     count = len(refs) // 2
     for src, dst in zip(refs[:count], refs[count:]):
         dst[...] = src[...]
+
+
+def settle(dm, _, mine, arrived, out, total, heard, sems):
+    u, step = dm.subs - 1, dm.third
+    inward, outward = [], []
+    for q in range(PIECES):
+        k = pl.ds(q * step, step)
+        inward.append(
+            (
+                pltpu.make_async_copy(mine.at[k], total.at[k], sems.at[q, 0]),
+                pltpu.make_async_copy(arrived.at[k], heard.at[k], sems.at[q, 1]),
+            )
+        )
+        outward.append(
+            [
+                pltpu.make_async_copy(
+                    total.at[k, pl.ds(e * BLK, BLK)],
+                    out.at[dm.towers - 1, k, pl.ds(e * dm.own + u * BLK, BLK)],
+                    sems.at[q, 2 + e],
+                )
+                for e in (0, 1)
+            ]
+        )
+    for copies in inward:
+        for copy in copies:
+            copy.start()
+    for q in range(PIECES):
+        for copy in inward[q]:
+            copy.wait()
+        k = pl.ds(q * step, step)
+        total[k] += heard[k].astype(F32)
+        for copy in outward[q]:
+            copy.start()
+    for copies in outward:
+        for copy in copies:
+            copy.wait()
 
 
 def fused(pooled, weight, fc_bias, stitch, cotangent, valid_mask, image_group, step_rate):
@@ -757,7 +805,7 @@
         for shape in (
             (4, NZ * NX), (2, 2), (NZ,), (2, NZ), (2, 3, 2), (2, 2, 3, 2), (2, 3, 2), (2, 2, 3, 2), (2,), (2, 2), (2,), (2, 2),
             (2, 3, 2), (2, 2, 3, 2), (2, 3, 2), (2, 2, 3, 2), (NZ, 2), (2, NZ, 2), (2,), (4, 2), (PIECES,), (2, PIECES), (3,), (3,),
-            (2,), (2,), (2, PIECES, 2), (), (2, 2), (2, 2),
+            (2,), (2,), (2, PIECES, 2), (), (2, 2), (2, 2), (PIECES, 2),
         )
     ]
     anyspace = pl.BlockSpec(memory_space=pl.ANY)
@@ -771,12 +819,13 @@
         jax.ShapeDtypeStruct((2, 2, BLK), F32),
     ]
     out_specs = [anyspace] * 3 + [inside] * 3
-    results = pl.pallas_call(
+    block = (feats, NX * BLK)
+    *results, mine, theirs = pl.pallas_call(
         functools.partial(kernel, dm),
         name="stitch_fc6",
-        out_shape=out_shape,
+        out_shape=out_shape + [jax.ShapeDtypeStruct(block, F32), jax.ShapeDtypeStruct(block, BF16)],
         in_specs=[pl.BlockSpec(memory_space=pltpu.SMEM)] + [anyspace] * 3 + [inside] * 4,
-        out_specs=out_specs,
+        out_specs=out_specs + [anyspace] * 2,
         scratch_shapes=scratch,
         compiler_params=pltpu.CompilerParams(collective_id=1, has_side_effects=True, vmem_limit_bytes=61 * 2**20),
         cost_estimate=pl.CostEstimate(
@@ -786,13 +835,15 @@
         step_rate, weight, pooled, cotangent, fc_bias, stitch,
         valid_mask.reshape(feats // BLK, BLK), image_group.reshape(images // BLK, BLK),
     )
-    def block(shape):
+    arrived = lax.ppermute(theirs, "batch", [(0, 2), (1, 3), (2, 0), (3, 1)])
+
+    def cut(shape):
         if len(shape.shape) == 3 and shape.shape[1] % (CUTS * 16) == 0:
             return pl.BlockSpec((shape.shape[0], shape.shape[1] // CUTS, shape.shape[2]), lambda c: (0, c, 0))
         return pl.BlockSpec(shape.shape, lambda c: (0,) * len(shape.shape))
 
-    blocks = [block(shape) for shape in out_shape]
-    return pl.pallas_call(
+    blocks = [cut(shape) for shape in out_shape]
+    results = pl.pallas_call(
         carry_out,
         name="carry_out",
         grid=(CUTS,),
@@ -800,7 +851,19 @@
         in_specs=blocks,
         out_specs=blocks,
         compiler_params=pltpu.CompilerParams(vmem_limit_bytes=60 * 2**20),
+        cost_estimate=pl.CostEstimate(flops=0, bytes_accessed=32 * 2**20, transcendentals=0),
     )(*results)
+    weight_grad = pl.pallas_call(
+        functools.partial(settle, dm),
+        name="settle",
+        out_shape=out_shape[2],
+        in_specs=[anyspace] * 3,
+        out_specs=anyspace,
+        scratch_shapes=[vm(block, F32), vm(block, BF16), dma((PIECES, 4))],
+        input_output_aliases={0: 0},
+        compiler_params=pltpu.CompilerParams(vmem_limit_bytes=6 * 2**20),
+    )(results[2], mine, arrived)
+    return *results[:2], weight_grad, *results[3:]
 
 
 def gelu_local(values):

time: 319 us -> 309 us (0.969)
  Pallas kernels: 317 us -> 303 us
  waiting for transfers between devices: 0 us -> 3.44 us
    pallas_call x1, Pallas kernels: 306 us -> 289 us  [fused(): pl.pallas_call(functools.partial(kernel, dm), name='stitch_fc6', out_shap...]
    ppermute x0 -> x1, waiting for transfers between devices: none -> 3.44 us  [fused(): arrived = lax.ppermute(theirs, 'batch', [(0, 2), (1, 3), (2, 0), (3, 1)])]
  transfers between devices with their start and end apart: 0 -> 1, of which waited for: 0 -> 1; matrix products, arithmetic and copies ran while one was open for 0% -> 0% of each run, Pallas kernels for 0% -> 4%
where the time goes in v5:
time: 309 us
  Pallas kernels  303 us (98%)
  waiting for transfers between devices  3.44 us (1%)
    pallas_call x1, Pallas kernels, fused(): pl.pallas_call(functools.partial(kernel, dm), name='stitch_fc6', out_shap...  289 us
    pallas_call x1, Pallas kernels, fused(): pl.pallas_call(carry_out, name='carry_out', grid=(CUTS,), out_shape=out_s...  11.3 us
  transfers between devices with their start and end apart: 1, of which 1 were waited for; matrix products, arithmetic and copies ran while one was open for 0% of the time, Pallas kernels for 4%

profile of v5, /device:TPU:0, one launch (start us, length us, event | category | flops | bytes accessed | tf_op | source)
XLA Modules:
  0.0 308.8 jit_solution(7427087722611494070)
XLA Ops:
  1.3 289.3 %stitch_fc6.1 = (bf16[2,512,1024]{2,1,0:T(8,128)(2,1)}, bf16[2,1152,1024]{2,1,0:T(8,128)(2,1)}, f32[2,1152,1024]{2,1,0:T(8,128)}, f32[2,128]{1,0:T(2,128)}, f32[...) custom-call(f32[1]{0:T(128)S(6)} %copy.16.step_ref, ...), custom_call_target="tpu_custom_call" | custom-call | flops 57982058496 | bytes 62914560 | tf_op jit(solution)/shard_map/stitch_fc6/pallas_call | solution.py:823
  290.6 0.9 collective-permute-start
  291.4 0.0 copy-start
  291.4 11.3 %carry_out.1 = (bf16[2,512,1024]{2,1,0:T(8,128)(2,1)}, bf16[2,1152,1024]{2,1,0:T(8,128)(2,1)}, f32[2,1152,1024]{2,1,0:T(8,128)}, f32[2,128]{1,0:T(2,128)}, f32[2,2,128]{2,1,0:T(2,128)}, /*index=5*/f32[2,2,128]{2,1,0:T(2,128)}) custom-call(bf16[2,512,1024]{2,1,0:T(8,128)(2,1)} %get-tuple-element.20.refs_0_, bf16[2,1152,1024]{2,1,0:T(8,128)(2,1)} %get-tuple-element.21.refs_1_, ...), custom_call_target="tpu_custom_call" | custom-call | bytes 33554432 | tf_op jit(solution)/shard_map/carry_out/pallas_call | solution.py:846
  302.8 3.4 %collective-permute-done.arrived = bf16[1152,256]{1,0:T(8,128)(2,1)S(1)} collective-permute-done((bf16[1152,256]{1,0:T(8,128)(2,1)}, bf16[1152,256]{1,0:T(8,128)(2,1)S(1)}, u32[]{:S(2)}, u32[]{:S(2)}) %collective-permute-start) | collective-permute-done | bytes 589856 | tf_op jit(solution)/shard_map/ppermute | solution.py:838
  306.2 0.0 copy-done
  306.2 2.5 settle.1
Async XLA Ops:
  290.6 15.6 %collective-permute-start = (bf16[1152,256]{1,0:T(8,128)(2,1)}, bf16[1152,256]{1,0:T(8,128)(2,1)S(1)}, u32[]{:S(2)}, u32[]{:S(2)}) collective-permute-start(bf16[1152,256]{1,0:T(8,128)(2,1)} %get-tuple-element.30), channel_id=1, source_target_pairs={{0,2},{1,3},{2,0},{3,1},{4,6},{5,7},{6,4},{7,5},{8,10},{9,11},{10,... | collective-permute-start | bytes 1769480 | tf_op jit(solution)/shard_map/ppermute | solution.py:838
  291.4 14.8 %copy-start = (f32[1152,256]{1,0:T(8,128)S(1)}, f32[1152,256]{1,0:T(8,128)}, u32[]{:S(2)}) copy-start(f32[1152,256]{1,0:T(8,128)} %get-tuple-element.29.mine) | copy-start | bytes 3538948

commit v6 on v5

--- a/solution.py
+++ b/solution.py
@@ -17,10 +17,12 @@
 CUBE = 0.044715
 PIECES = 3
 CUTS = 4
+TAILX = 30
 DRAIN = (
-    "zf0", "xf0", "zf1", "xf1", "hz00", "hz01", "bv0", "gs0", "gx00", "gs1", "gx01", "hz10", "hz11", "bv1", "em",
-    "gz00", "gx10", "gz01", "gx11", "hz20", "hz21", "hd", "bv2", "gz10", "gx20", "gz11", "gx21", "hp0", "hp1", "hp2",
-    "ss", "bw0", "bw1", "bw2", "gz20", "gz21", "gd", "bp0", "bp1", "bp2", "bx0", "bx1", "bx2",
+    "zf0", "zf1", "sz0", "sz1", "xf0", "xf1", "sx0", "sx1", "bv0", "hz00", "hz01", "bv1", "gs0", "gx00", "gs1", "gx01",
+    "hz10", "hz11", "bv2", "em", "gz00", "gx10", "gz01", "gx11", "hz20", "hz21", "hd", "gz10", "gx20", "gz11", "gx21",
+    "hp0", "hp1", "hp2", "ss", "bw0", "bw1", "bw2", "gz20", "gz21", "gd", "bp0", "bp1", "bp2", "ya0", "bx0", "ya1",
+    "bx1", "bx2", "ya2",
 )
 ORDER = (
     "zr00", "ws", "zf0", "gz00", "bw0", "x10", "xf0", "ww", "p0", "zr01", "zf1", "gz01", "bw1", "xf1", "f0",
@@ -64,6 +66,10 @@
     mid_x, mid_z = rx // 32 * 16, rz // 32 * 16
     cuts_x = (0, mid_x), (mid_x, rx - mid_x)
     cuts_z = (0, mid_z), (mid_z, rz - mid_z)
+    late = rows * TAILX // 32 // 32 * 32
+    rest = (rows - late) // 32 * 16
+    tail_x = (0, late // 2), (late // 2, late // 2)
+    tail_z = (late - rx, rest), (late - rx + rest, rows - late - rest)
     wi, bi = lax.axis_index("wide"), lax.axis_index("batch")
     z, x = wi // NX, wi % NX
     y, core = bi // 2, bi % 2
@@ -136,12 +142,15 @@
         cut = pl.ds(*cuts_z[f])
         return rc(z2_s.at[cut], z2_r.at[n % 2, cut], m_z2s.at[f], m_z2r.at[n % 2, f], x_dev)
 
+    def final(n):
+        return isinstance(n, int) and n == n_units - 1
+
     def g_x(n, o, xx, f):
-        start, size = cuts_x[f]
+        start, size = tail_x[f] if final(n) else cuts_x[f]
         return gat.at[gpair(n), pl.ds(al(part(n) * rows + start, 16), size), pl.ds(col(o, xx), BLK)]
 
     def g_z(n, o, xx, width, f):
-        start, size = cuts_z[f]
+        start, size = tail_z[f] if final(n) else cuts_z[f]
         return gat.at[gpair(n), pl.ds(al(part(n) * rows + rx + start, 16), size), pl.ds(col(o, xx), width)]
 
     def z4_copy(n, f):
@@ -170,7 +179,7 @@
 
     def y_copy(p, q):
         k = pl.ds(q * dm.third, dm.third)
-        return rc(y_s.at[k], y_r.at[p % 2, k], m_ys.at[q], m_yr.at[p % 2, q], y_dev)
+        return rc(y_s.at[p % 2, k], y_r.at[p % 2, k], m_ys.at[p % 2, q], m_yr.at[p % 2, q], y_dev)
 
     def own_copy(p, q, e):
         t, u = p // dm.subs, p % dm.subs
@@ -182,10 +191,11 @@
         )
 
     def last_copies(q):
+        slot = (dm.towers * dm.subs - 1) % 2
         k = pl.ds(q * dm.third, dm.third)
         return (
-            pltpu.make_async_copy(y_s.at[k], theirs_hbm.at[k], m_last.at[q, 0]),
-            pltpu.make_async_copy(own.at[(dm.towers * dm.subs - 1) % 2, k], mine_hbm.at[k], m_last.at[q, 1]),
+            pltpu.make_async_copy(y_s.at[slot, k], theirs_hbm.at[k], m_last.at[q, 0]),
+            pltpu.make_async_copy(own.at[slot, k], mine_hbm.at[k], m_last.at[q, 1]),
         )
 
     def pg_copy(t, s):
@@ -373,13 +383,21 @@
             return zown[r : r + m] + z2_r[n % 2, r : r + m].astype(F32)
 
         finish(n, rx + start, size, total)
-
+        if not final(n):
+            z4_send(n, f)
+        mix(n, rx + start, size)
+
+    def z4_send(n, f):
         @pl.when(n >= 1)
         def _():
-            z4_copy(n, f).wait_send()
+            z4_copy(n - 1, f).wait_send()
 
         z4_copy(n, f).start()
-        mix(n, rx + start, size)
+
+    def gx_send(n, f):
+        for d in (0, 1):
+            gather_hop(gx_copy, n, d, 0, f)
+        x5_send(n, z, f)
 
     def x_final(n, f):
         if f == 0:
@@ -401,9 +419,8 @@
             )
 
         finish(n, start, size, total)
-        for d in (0, 1):
-            gather_hop(gx_copy, n, d, 0, f)
-        x5_send(n, z, f)
+        if not final(n):
+            gx_send(n, f)
         mix(n, start, size)
 
     def gather_hop(copy, n, d, h, f):
@@ -411,14 +428,14 @@
         def _():
             @pl.when(n >= 1)
             def _():
-                copy(n, d, h, f).wait_send()
+                copy(n - 1, d, h, f).wait_send()
 
             copy(n, d, h, f).start()
 
     def x5_send(n, o, f):
         @pl.when(n >= 1)
         def _():
-            x5_copy(n, o, x, f).wait_send()
+            x5_copy(n - 1, o, x, f).wait_send()
 
         x5_copy(n, o, x, f).start()
 
@@ -486,7 +503,7 @@
 
     def back_weight(n, q):
         t, s, p = tower(n), part(n), n // dm.parts
-        is_last = isinstance(n, int) and n == n_units - 1
+        is_last = final(n)
         k, imgs = pl.ds(q * dm.third, dm.third), pl.ds(al(part(n) * rows), rows)
         if q == 0:
             for e in (0, 1):
@@ -504,9 +521,10 @@
 
         @pl.when(s == 0)
         def _():
-            @pl.when(p >= 1)
-            def _():
-                y_arrive(p - 1, q)
+            if not isinstance(n, int):
+                @pl.when(p >= 1)
+                def _():
+                    y_arrive(p - 1, q)
 
             @pl.when(p >= 2)
             def _():
@@ -518,11 +536,11 @@
 
         @pl.when(s == 1)
         def _():
-            @pl.when(p >= 1)
-            def _():
-                y_copy(p - 1, q).wait_send()
-
-            y_s[k, :] = (tacc[k, :] + grads(1 - y)).astype(BF16)
+            @pl.when(p >= 2)
+            def _():
+                y_copy(p - 2, q).wait_send()
+
+            y_s[p % 2, k, :] = (tacc[k, :] + grads(1 - y)).astype(BF16)
             if not is_last:
                 y_copy(p, q).start()
             own[p % 2, k, :] += grads(y)
@@ -541,6 +559,33 @@
     x_load(0, 0).start()
     for w in range(NZ * NX):
         w_load(0, w).start()
+    barrier = pltpu.get_barrier_semaphore()
+    peers = [x_dev] + [(wi, lax.rem(bi + k, 4)) for k in (1, 2, 3)]
+    for dev in peers:
+        pl.semaphore_signal(barrier, inc=1, device_id=dev, device_id_type=MESH)
+    for d in (0, 1):
+        @pl.when(far(d) <= 2)
+        def _():
+            pl.semaphore_signal(barrier, inc=1, device_id=z_dev(d), device_id_type=MESH)
+
+    small_img[...] = jnp.concatenate([group[j : j + 1] for j in range(dm.images // BLK)], axis=1).astype(F32)
+    for j in range(dm.feats // BLK):
+        gap = 1.0 - valid[j : j + 1].astype(F32)
+        hole[j * BLK : (j + 1) * BLK] = jnp.broadcast_to(gap, (BLK, BLK)).T
+    x_load(0, 0).wait()
+    prepare(0, 0)
+
+    for d in (0, 1):
+        @pl.when(far(d) == 0)
+        def _():
+            for s in (0, 1):
+                for h in range(3):
+                    xr_r[s, d, h] = jnp.zeros((rx, BLK), BF16)
+                    zr_r[s, d, h] = jnp.zeros((rz, NX * BLK), BF16)
+
+    pl.semaphore_wait(barrier, jnp.where((z == 0) | (z == NZ - 1), len(peers) + 1, len(peers) + 2))
+    for w in range(NZ * NX):
+        w_load(0, w).wait()
     x_load(0, 1).start()
     for i in (0, 1):
         cot_load(0, i).start()
@@ -549,33 +594,6 @@
     for s in (0, 1):
         x_load(1, s).start()
 
-    barrier = pltpu.get_barrier_semaphore()
-    peers = [x_dev] + [(wi, lax.rem(bi + k, 4)) for k in (1, 2, 3)]
-    for dev in peers:
-        pl.semaphore_signal(barrier, inc=1, device_id=dev, device_id_type=MESH)
-    for d in (0, 1):
-        @pl.when(far(d) <= 2)
-        def _():
-            pl.semaphore_signal(barrier, inc=1, device_id=z_dev(d), device_id_type=MESH)
-
-    small_img[...] = jnp.concatenate([group[j : j + 1] for j in range(dm.images // BLK)], axis=1).astype(F32)
-    for j in range(dm.feats // BLK):
-        gap = 1.0 - valid[j : j + 1].astype(F32)
-        hole[j * BLK : (j + 1) * BLK] = jnp.broadcast_to(gap, (BLK, BLK)).T
-    x_load(0, 0).wait()
-    prepare(0, 0)
-
-    for d in (0, 1):
-        @pl.when(far(d) == 0)
-        def _():
-            for s in (0, 1):
-                for h in range(3):
-                    xr_r[s, d, h] = jnp.zeros((rx, BLK), BF16)
-                    zr_r[s, d, h] = jnp.zeros((rz, NX * BLK), BF16)
-
-    pl.semaphore_wait(barrier, jnp.where((z == 0) | (z == NZ - 1), len(peers) + 1, len(peers) + 2))
-    for w in range(NZ * NX):
-        w_load(0, w).wait()
     for k in range(4):
         forward(0, k)
     sacc[...] = jnp.zeros_like(sacc)
@@ -660,6 +678,7 @@
         "ss": sums_send,
     }
     for q in range(PIECES):
+        ends[f"ya{q}"] = functools.partial(y_arrive, pairs - 2, q)
         ends[f"bv{q}"] = functools.partial(back_weight, last - 2, q)
         ends[f"bw{q}"] = functools.partial(back_weight, last - 1, q)
         ends[f"bx{q}"] = functools.partial(back_weight, last, q)
@@ -668,6 +687,8 @@
     for f in (0, 1):
         ends[f"zf{f}"] = functools.partial(z_final, last, f)
         ends[f"xf{f}"] = functools.partial(x_final, last, f)
+        ends[f"sz{f}"] = functools.partial(z4_send, last, f)
+        ends[f"sx{f}"] = functools.partial(gx_send, last, f)
         ends[f"gs{f}"] = functools.partial(gz_first, last, f)
         for h in range(3):
             ends[f"gx{h}{f}"] = functools.partial(gather_arrive, gx_copy, last, h, True, f)
@@ -688,6 +709,7 @@
             own_copy(pairs - 2, q, e).wait()
         for copy in last_copies(q):
             copy.wait()
+        y_copy(pairs - 2, q).wait_send()
     pg_copy(1, 1).wait()
     for i in (0, 1):
         s_copy(last - 1, i).wait()
@@ -724,40 +746,23 @@
         dst[...] = src[...]
 
 
-def settle(dm, _, mine, arrived, out, total, heard, sems):
+def settle(dm, _, mine, arrived, out, total, sems):
     u, step = dm.subs - 1, dm.third
-    inward, outward = [], []
+    copies = []
     for q in range(PIECES):
         k = pl.ds(q * step, step)
-        inward.append(
-            (
-                pltpu.make_async_copy(mine.at[k], total.at[k], sems.at[q, 0]),
-                pltpu.make_async_copy(arrived.at[k], heard.at[k], sems.at[q, 1]),
-            )
-        )
-        outward.append(
-            [
+        total[k] = mine[k] + arrived[k].astype(F32)
+        for e in (0, 1):
+            copies.append(
                 pltpu.make_async_copy(
                     total.at[k, pl.ds(e * BLK, BLK)],
                     out.at[dm.towers - 1, k, pl.ds(e * dm.own + u * BLK, BLK)],
-                    sems.at[q, 2 + e],
+                    sems.at[q, e],
                 )
-                for e in (0, 1)
-            ]
-        )
-    for copies in inward:
-        for copy in copies:
-            copy.start()
-    for q in range(PIECES):
-        for copy in inward[q]:
-            copy.wait()
-        k = pl.ds(q * step, step)
-        total[k] += heard[k].astype(F32)
-        for copy in outward[q]:
-            copy.start()
-    for copies in outward:
-        for copy in copies:
-            copy.wait()
+            )
+            copies[-1].start()
+    for copy in copies:
+        copy.wait()
 
 
 def fused(pooled, weight, fc_bias, stitch, cotangent, valid_mask, image_group, step_rate):
@@ -792,7 +797,7 @@
         vm((2, rz, BLK), BF16),
         vm((2, feats, NX * BLK), F32),
         vm((feats, NX * BLK), F32),
-        vm((feats, NX * BLK), BF16),
+        vm((2, feats, NX * BLK), BF16),
         vm((2, feats, NX * BLK), BF16),
         vm((images, own), F32),
         vm((max(rx, rz), BLK), F32),
@@ -804,7 +809,7 @@
         dma(shape)
         for shape in (
             (4, NZ * NX), (2, 2), (NZ,), (2, NZ), (2, 3, 2), (2, 2, 3, 2), (2, 3, 2), (2, 2, 3, 2), (2,), (2, 2), (2,), (2, 2),
-            (2, 3, 2), (2, 2, 3, 2), (2, 3, 2), (2, 2, 3, 2), (NZ, 2), (2, NZ, 2), (2,), (4, 2), (PIECES,), (2, PIECES), (3,), (3,),
+            (2, 3, 2), (2, 2, 3, 2), (2, 3, 2), (2, 2, 3, 2), (NZ, 2), (2, NZ, 2), (2,), (4, 2), (2, PIECES), (2, PIECES), (3,), (3,),
             (2,), (2,), (2, PIECES, 2), (), (2, 2), (2, 2), (PIECES, 2),
         )
     ]
@@ -857,9 +862,9 @@
         functools.partial(settle, dm),
         name="settle",
         out_shape=out_shape[2],
-        in_specs=[anyspace] * 3,
+        in_specs=[anyspace, inside, inside],
         out_specs=anyspace,
-        scratch_shapes=[vm(block, F32), vm(block, BF16), dma((PIECES, 4))],
+        scratch_shapes=[vm(block, F32), dma((PIECES, 2))],
         input_output_aliases={0: 0},
         compiler_params=pltpu.CompilerParams(vmem_limit_bytes=6 * 2**20),
     )(results[2], mine, arrived)

time: 309 us -> 306 us (level)
  no operation moved by 1% of the time
where the time goes in v6:
time: 306 us; the launch traced here: 305 us
  Pallas kernels  300 us (98%)
    pallas_call x1, Pallas kernels, fused(): pl.pallas_call(functools.partial(kernel, dm), name='stitch_fc6', out_shap...  287 us
    pallas_call x1, Pallas kernels, fused(): pl.pallas_call(carry_out, name='carry_out', grid=(CUTS,), out_shape=out_s...  11.3 us
  transfers between devices with their start and end apart: 1, of which 1 were waited for; matrix products, arithmetic and copies ran while one was open for 0% of the time, Pallas kernels for 4%

profile of v6, /device:TPU:0, one launch (start us, length us, event | category | flops | bytes accessed | tf_op | source)
XLA Modules:
  0.0 305.4 jit_solution(3292598771416010425)
XLA Ops:
  1.3 287.2 %stitch_fc6.1 = (bf16[2,512,1024]{2,1,0:T(8,128)(2,1)}, bf16[2,1152,1024]{2,1,0:T(8,128)(2,1)}, f32[2,1152,1024]{2,1,0:T(8,128)}, f32[2,128]{1,0:T(2,128)}, f32[...) custom-call(f32[1]{0:T(128)S(6)} %copy.16.step_ref, ...), custom_call_target="tpu_custom_call" | custom-call | flops 57982058496 | bytes 62914560 | tf_op jit(solution)/shard_map/stitch_fc6/pallas_call | solution.py:828
  288.5 1.6 collective-permute-start
  290.1 0.0 copy-start
  290.1 11.3 %carry_out.1 = (bf16[2,512,1024]{2,1,0:T(8,128)(2,1)}, bf16[2,1152,1024]{2,1,0:T(8,128)(2,1)}, f32[2,1152,1024]{2,1,0:T(8,128)}, f32[2,128]{1,0:T(2,128)}, f32[2,2,128]{2,1,0:T(2,128)}, /*index=5*/f32[2,2,128]{2,1,0:T(2,128)}) custom-call(bf16[2,512,1024]{2,1,0:T(8,128)(2,1)} %get-tuple-element.20.refs_0_, bf16[2,1152,1024]{2,1,0:T(8,128)(2,1)} %get-tuple-element.21.refs_1_, ...), custom_call_target="tpu_custom_call" | custom-call | bytes 33554432 | tf_op jit(solution)/shard_map/carry_out/pallas_call | solution.py:851
  301.4 2.7 collective-permute-done.arrived
  304.1 0.0 copy-done
  304.1 1.1 settle.1
Async XLA Ops:
  288.5 15.6 %collective-permute-start = (bf16[1152,256]{1,0:T(8,128)(2,1)}, bf16[1152,256]{1,0:T(8,128)(2,1)S(1)}, u32[]{:S(2)}, u32[]{:S(2)}) collective-permute-start(bf16[1152,256]{1,0:T(8,128)(2,1)} %get-tuple-element.30), channel_id=1, source_target_pairs={{0,2},{1,3},{2,0},{3,1},{4,6},{5,7},{6,4},{7,5},{8,10},{9,11},{10,... | collective-permute-start | bytes 1769480 | tf_op jit(solution)/shard_map/ppermute | solution.py:843
  290.1 14.0 %copy-start = (f32[1152,256]{1,0:T(8,128)S(1)}, f32[1152,256]{1,0:T(8,128)}, u32[]{:S(2)}) copy-start(f32[1152,256]{1,0:T(8,128)} %get-tuple-element.29.mine) | copy-start | bytes 3538948

commit v7 on v6

--- a/solution.py
+++ b/solution.py
@@ -19,16 +19,16 @@
 CUTS = 4
 TAILX = 30
 DRAIN = (
-    "zf0", "zf1", "sz0", "sz1", "xf0", "xf1", "sx0", "sx1", "bv0", "hz00", "hz01", "bv1", "gs0", "gx00", "gs1", "gx01",
-    "hz10", "hz11", "bv2", "em", "gz00", "gx10", "gz01", "gx11", "hz20", "hz21", "hd", "gz10", "gx20", "gz11", "gx21",
+    "hz00", "hz01", "zf0", "zf1", "sz0", "sz1", "xf0", "xf1", "sx0", "sx1", "bv0", "gs0", "gs1", "hz10", "hz11", "gx00",
+    "gx01", "bv1", "gz00", "gz01", "gx10", "gx11", "hz20", "hz21", "bv2", "gz10", "gz11", "gx20", "gx21", "hd", "em",
     "hp0", "hp1", "hp2", "ss", "bw0", "bw1", "bw2", "gz20", "gz21", "gd", "bp0", "bp1", "bp2", "ya0", "bx0", "ya1",
     "bx1", "bx2", "ya2",
 )
 ORDER = (
-    "zr00", "ws", "zf0", "gz00", "bw0", "x10", "xf0", "ww", "p0", "zr01", "zf1", "gz01", "bw1", "xf1", "f0",
-    "zr10", "gz10", "f1", "x11", "xr00", "gx00", "em", "zr11", "gz11", "bw2", "xr01", "gx01", "f2",
-    "zr20", "gz20", "ct", "az", "x12", "xr10", "gx10", "f3", "zr21", "gz21", "gd", "bp0", "xr11", "gx11",
-    "zs0", "gs0", "x13", "xr20", "gx20", "bp1", "zs1", "gs1", "bp2", "xr21", "gx21",
+    "zr00", "ws", "zf0", "gz00", "bw0", "x10", "xf0", "ww", "p0", "zr01", "zf1", "gz01", "xf1", "x11", "f0",
+    "zr10", "gz10", "bw1", "xr00", "gx00", "em", "zr11", "gz11", "f1", "xr01", "gx01", "x12", "f2",
+    "zr20", "gz20", "bw2", "ct", "az", "xr10", "gx10", "f3", "zr21", "gz21", "gd", "bp0", "xr11", "gx11", "x13",
+    "zs0", "gs0", "xr20", "gx20", "bp1", "zs1", "gs1", "bp2", "xr21", "gx21",
 )
 
 

time: 306 us -> 304 us (level)
  no operation moved by 1% of the time
where the time goes in v7:
time: 304 us
  Pallas kernels  298 us (98%)
    pallas_call x1, Pallas kernels, fused(): pl.pallas_call(functools.partial(kernel, dm), name='stitch_fc6', out_shap...  285 us
    pallas_call x1, Pallas kernels, fused(): pl.pallas_call(carry_out, name='carry_out', grid=(CUTS,), out_shape=out_s...  11.3 us
  transfers between devices with their start and end apart: 1, of which 1 were waited for; matrix products, arithmetic and copies ran while one was open for 0% of the time, Pallas kernels for 4%

profile of v7, /device:TPU:0, one launch (start us, length us, event | category | flops | bytes accessed | tf_op | source)
XLA Modules:
  0.0 303.5 jit_solution(12432473868871530281)
XLA Ops:
  1.3 285.4 %stitch_fc6.1 = (bf16[2,512,1024]{2,1,0:T(8,128)(2,1)}, bf16[2,1152,1024]{2,1,0:T(8,128)(2,1)}, f32[2,1152,1024]{2,1,0:T(8,128)}, f32[2,128]{1,0:T(2,128)}, f32[...) custom-call(f32[1]{0:T(128)S(6)} %copy.16.step_ref, ...), custom_call_target="tpu_custom_call" | custom-call | flops 57982058496 | bytes 62914560 | tf_op jit(solution)/shard_map/stitch_fc6/pallas_call | solution.py:828
  286.7 1.4 collective-permute-start
  288.1 0.0 copy-start
  288.1 11.3 %carry_out.1 = (bf16[2,512,1024]{2,1,0:T(8,128)(2,1)}, bf16[2,1152,1024]{2,1,0:T(8,128)(2,1)}, f32[2,1152,1024]{2,1,0:T(8,128)}, f32[2,128]{1,0:T(2,128)}, f32[2,2,128]{2,1,0:T(2,128)}, /*index=5*/f32[2,2,128]{2,1,0:T(2,128)}) custom-call(bf16[2,512,1024]{2,1,0:T(8,128)(2,1)} %get-tuple-element.20.refs_0_, bf16[2,1152,1024]{2,1,0:T(8,128)(2,1)} %get-tuple-element.21.refs_1_, ...), custom_call_target="tpu_custom_call" | custom-call | bytes 33554432 | tf_op jit(solution)/shard_map/carry_out/pallas_call | solution.py:851
  299.5 2.8 collective-permute-done.arrived
  302.3 0.0 copy-done
  302.3 1.1 settle.1
Async XLA Ops:
  286.7 15.6 %collective-permute-start = (bf16[1152,256]{1,0:T(8,128)(2,1)}, bf16[1152,256]{1,0:T(8,128)(2,1)S(1)}, u32[]{:S(2)}, u32[]{:S(2)}) collective-permute-start(bf16[1152,256]{1,0:T(8,128)(2,1)} %get-tuple-element.30), channel_id=1, source_target_pairs={{0,2},{1,3},{2,0},{3,1},{4,6},{5,7},{6,4},{7,5},{8,10},{9,11},{10,... | collective-permute-start | bytes 1769480 | tf_op jit(solution)/shard_map/ppermute | solution.py:843
  288.1 14.1 %copy-start = (f32[1152,256]{1,0:T(8,128)S(1)}, f32[1152,256]{1,0:T(8,128)}, u32[]{:S(2)}) copy-start(f32[1152,256]{1,0:T(8,128)} %get-tuple-element.29.mine) | copy-start | bytes 3538948

commit v8 on v7

--- a/solution.py
+++ b/solution.py
@@ -25,7 +25,7 @@
     "bx1", "bx2", "ya2",
 )
 ORDER = (
-    "zr00", "ws", "zf0", "gz00", "bw0", "x10", "xf0", "ww", "p0", "zr01", "zf1", "gz01", "xf1", "x11", "f0",
+    "x10", "zr00", "ws", "zf0", "gz00", "bw0", "xf0", "ww", "p0", "zr01", "zf1", "gz01", "xf1", "x11", "f0",
     "zr10", "gz10", "bw1", "xr00", "gx00", "em", "zr11", "gz11", "f1", "xr01", "gx01", "x12", "f2",
     "zr20", "gz20", "bw2", "ct", "az", "xr10", "gx10", "f3", "zr21", "gz21", "gd", "bp0", "xr11", "gx11", "x13",
     "zs0", "gs0", "xr20", "gx20", "bp1", "zs1", "gs1", "bp2", "xr21", "gx21",

time: 304 us -> 304 us (level)
  no operation moved by 1% of the time
where the time goes in v8:
time: 304 us
  Pallas kernels  298 us (98%)
    pallas_call x1, Pallas kernels, fused(): pl.pallas_call(functools.partial(kernel, dm), name='stitch_fc6', out_shap...  286 us
    pallas_call x1, Pallas kernels, fused(): pl.pallas_call(carry_out, name='carry_out', grid=(CUTS,), out_shape=out_s...  11.3 us
  transfers between devices with their start and end apart: 1, of which 1 were waited for; matrix products, arithmetic and copies ran while one was open for 0% of the time, Pallas kernels for 4%

profile of v8, /device:TPU:0, one launch (start us, length us, event | category | flops | bytes accessed | tf_op | source)
XLA Modules:
  0.0 303.9 jit_solution(2563578451497959038)
XLA Ops:
  1.3 285.8 %stitch_fc6.1 = (bf16[2,512,1024]{2,1,0:T(8,128)(2,1)}, bf16[2,1152,1024]{2,1,0:T(8,128)(2,1)}, f32[2,1152,1024]{2,1,0:T(8,128)}, f32[2,128]{1,0:T(2,128)}, f32[...) custom-call(f32[1]{0:T(128)S(6)} %copy.16.step_ref, ...), custom_call_target="tpu_custom_call" | custom-call | flops 57982058496 | bytes 62914560 | tf_op jit(solution)/shard_map/stitch_fc6/pallas_call | solution.py:828
  287.1 1.6 collective-permute-start
  288.7 0.0 copy-start
  288.7 11.3 %carry_out.1 = (bf16[2,512,1024]{2,1,0:T(8,128)(2,1)}, bf16[2,1152,1024]{2,1,0:T(8,128)(2,1)}, f32[2,1152,1024]{2,1,0:T(8,128)}, f32[2,128]{1,0:T(2,128)}, f32[2,2,128]{2,1,0:T(2,128)}, /*index=5*/f32[2,2,128]{2,1,0:T(2,128)}) custom-call(bf16[2,512,1024]{2,1,0:T(8,128)(2,1)} %get-tuple-element.20.refs_0_, bf16[2,1152,1024]{2,1,0:T(8,128)(2,1)} %get-tuple-element.21.refs_1_, ...), custom_call_target="tpu_custom_call" | custom-call | bytes 33554432 | tf_op jit(solution)/shard_map/carry_out/pallas_call | solution.py:851
  300.0 2.7 collective-permute-done.arrived
  302.7 0.0 copy-done
  302.7 1.1 settle.1
Async XLA Ops:
  287.1 15.6 %collective-permute-start = (bf16[1152,256]{1,0:T(8,128)(2,1)}, bf16[1152,256]{1,0:T(8,128)(2,1)S(1)}, u32[]{:S(2)}, u32[]{:S(2)}) collective-permute-start(bf16[1152,256]{1,0:T(8,128)(2,1)} %get-tuple-element.30), channel_id=1, source_target_pairs={{0,2},{1,3},{2,0},{3,1},{4,6},{5,7},{6,4},{7,5},{8,10},{9,11},{10,... | collective-permute-start | bytes 1769480 | tf_op jit(solution)/shard_map/ppermute | solution.py:843
  288.7 14.0 %copy-start = (f32[1152,256]{1,0:T(8,128)S(1)}, f32[1152,256]{1,0:T(8,128)}, u32[]{:S(2)}) copy-start(f32[1152,256]{1,0:T(8,128)} %get-tuple-element.29.mine) | copy-start | bytes 3538948
